TPU v7x, 128 devices: a whole 4x4x4 slice. The times are simulated.
128 devices in a mesh: expert: 16 (over z, y), tensor: 8 (over x, core).
Axes of the slice: x: 4, y: 4, z: 4, core: 2. Of those that a mesh axis runs over, the one named last changes fastest.
Arguments:
- context: bfloat16 [16384, 4096], P('expert', 'tensor'), may hold values from -6 to 6
- out_proj: bfloat16 [4096, 2880], P('tensor'), may hold values from -0.09375 to 0.09375
- residual_in: bfloat16 [16384, 2880], P(('expert', 'tensor')), may hold values from -36 to 36
- gain: bfloat16 [2880], replicated, may hold values from 0.099609375 to 1.8984375
- up_weight: bfloat16 [128, 2880, 1440], P(('expert', 'tensor')), may hold values from -0.109375 to 0.109375
- down_weight: bfloat16 [128, 1440, 2880], P(('expert', 'tensor')), may hold values from -0.15625 to 0.15625
- expert_ids: int32 [16384, 4], P(('expert', 'tensor')), may hold values from 0 to 127, all different within a row; in each aligned block of 128 rows (0 to 127, 128 to 255, ...) at most 5 rows name the same one
- gate_counts: int32 [16384, 4], P(('expert', 'tensor')), may hold values from 1 to 8
- grad_out: bfloat16 [16384, 2880], P(('expert', 'tensor')), may hold values from -6 to 6
Outputs:
- mixed: bfloat16 [16384, 2880], P(('expert', 'tensor'))
- grad_residual: bfloat16 [16384, 2880], P(('expert', 'tensor'))
- grad_context: bfloat16 [16384, 4096], P('expert', 'tensor')
Inputs may be any that keep to these rules, and one draw needn't show every extreme that they name: `expert_ids`: each row names 4 different experts. Among the 128 rows of one device no expert is named more than 5 times, a bound that some block reaches.
All inputs are finite; a program needn't handle non-finite values.
Results may differ from a plain program's by a relative error of at most 0.011.
Values may be sent and summed in bfloat16 or wider, within the bound.
A program may use at most 192 MiB of HBM per device.

v0:
```python
import jax
import jax.numpy as jnp
from jax import lax
from jax.sharding import PartitionSpec as P


def silu_slope(pre_act):
    sigmoid_value = jax.nn.sigmoid(pre_act)
    return sigmoid_value * (1.0 + pre_act * (1.0 - sigmoid_value))


def local(
    context, out_proj, residual_in, gain, up_weight, down_weight, expert_ids, gate_counts, grad_out
):
    tok_rows, width = residual_in.shape
    top_k = expert_ids.shape[1]
    n_expert = lax.axis_size("expert")
    n_tensor = lax.axis_size("tensor")
    experts = n_expert * n_tensor
    capacity = max(2, -(-(tok_rows * top_k * 5) // (4 * experts)))
    attention = lax.psum_scatter(
        jnp.dot(context, out_proj, preferred_element_type=jnp.float32).astype(jnp.bfloat16),
        "tensor",
        scatter_dimension=0,
        tiled=True,
    ).astype(jnp.float32)
    hidden_in = residual_in.astype(jnp.float32) + attention
    inv_rms = lax.rsqrt(jnp.mean(hidden_in * hidden_in, axis=1, keepdims=True) + 1e-05)
    gain_f = gain.astype(jnp.float32)
    normed = (hidden_in * inv_rms * gain_f).astype(jnp.bfloat16)
    counts = gate_counts.astype(jnp.float32)
    weights = counts / jnp.sum(counts, axis=1, keepdims=True)
    routed_ids = expert_ids.reshape(-1)
    onehot = (routed_ids[:, None] == jnp.arange(experts, dtype=jnp.int32)[None, :]).astype(
        jnp.int32
    )
    earlier = jnp.cumsum(onehot, axis=0) - onehot
    slot_rank = jnp.sum(earlier * onehot, axis=1)
    positions = routed_ids * capacity + slot_rank
    token_ids = jnp.arange(tok_rows * top_k, dtype=jnp.int32) // top_k
    grad_f = grad_out.astype(jnp.float32)
    scaled = (weights.reshape(-1)[:, None] * grad_f[token_ids]).astype(jnp.bfloat16)
    send_normed = (
        jnp.zeros((experts * capacity, width), jnp.bfloat16).at[positions].set(normed[token_ids])
    )
    send_scaled = jnp.zeros((experts * capacity, width), jnp.bfloat16).at[positions].set(scaled)
    send_normed = send_normed.reshape(experts, capacity, width)
    send_scaled = send_scaled.reshape(experts, capacity, width)
    got_normed, got_scaled = (
        lax.all_to_all(send_normed, ("expert", "tensor"), split_axis=0, concat_axis=0, tiled=True),
        lax.all_to_all(send_scaled, ("expert", "tensor"), split_axis=0, concat_axis=0, tiled=True),
    )
    inputs = got_normed.reshape(experts * capacity, width)
    cotangents = got_scaled.reshape(experts * capacity, width)
    up_rows = up_weight[0]
    down_rows = down_weight[0]
    pre_act = jnp.dot(inputs, up_rows, preferred_element_type=jnp.float32)
    activated = jax.nn.silu(pre_act).astype(jnp.bfloat16)
    expert_out = jnp.dot(activated, down_rows, preferred_element_type=jnp.float32).astype(
        jnp.bfloat16
    )
    back_hidden = jnp.einsum("rd,fd->rf", cotangents, down_rows, preferred_element_type=jnp.float32)
    grad_pre = (back_hidden * silu_slope(pre_act)).astype(jnp.bfloat16)
    grad_route = jnp.einsum(
        "rf,df->rd", grad_pre, up_rows, preferred_element_type=jnp.float32
    ).astype(jnp.bfloat16)
    back_out, back_grad = (
        lax.all_to_all(
            expert_out.reshape(experts, capacity, width),
            ("expert", "tensor"),
            split_axis=0,
            concat_axis=0,
            tiled=True,
        ),
        lax.all_to_all(
            grad_route.reshape(experts, capacity, width),
            ("expert", "tensor"),
            split_axis=0,
            concat_axis=0,
            tiled=True,
        ),
    )
    out_routes = back_out.reshape(experts * capacity, width)[positions].reshape(
        tok_rows, top_k, width
    )
    expert_mix = jnp.einsum("tk,tkd->td", weights, out_routes.astype(jnp.float32))
    mixed = (hidden_in + expert_mix).astype(jnp.bfloat16)
    grad_routes = back_grad.reshape(experts * capacity, width)[positions].reshape(
        tok_rows, top_k, width
    )
    grad_normed = jnp.sum(grad_routes.astype(jnp.float32), axis=1)
    scaled_grad = grad_normed * gain_f
    grad_hidden = (
        grad_f
        + inv_rms * scaled_grad
        - hidden_in * inv_rms**3 * jnp.mean(hidden_in * scaled_grad, axis=1, keepdims=True)
    )
    grad_residual = grad_hidden.astype(jnp.bfloat16)
    grad_context = jnp.einsum(
        "td,cd->tc",
        lax.all_gather(grad_residual, "tensor", axis=0, tiled=True),
        out_proj,
        preferred_element_type=jnp.float32,
    ).astype(jnp.bfloat16)
    return (mixed, grad_residual, grad_context)


def solution(mesh):
    in_specs = (
        P("expert", "tensor"),
        P("tensor", None),
        P(("expert", "tensor"), None),
        P(),
        P(("expert", "tensor"), None, None),
        P(("expert", "tensor"), None, None),
        P(("expert", "tensor"), None),
        P(("expert", "tensor"), None),
        P(("expert", "tensor"), None),
    )
    out_specs = (
        P(("expert", "tensor"), None),
        P(("expert", "tensor"), None),
        P("expert", "tensor"),
    )
    return jax.shard_map(local, mesh=mesh, in_specs=in_specs, out_specs=out_specs, check_vma=False)
```

profile of v0, /device:TPU:1, one launch (start us, length us, event | category | flops | bytes accessed | tf_op | source)
XLA Modules:
  0.0 522.1 jit_solution(5987616043298062887)
XLA Ops:
  7.2 1.8 copy-done
  9.0 6.3 %convolution_convert_fusion = bf16[1024,2880]{0,1:T(8,128)(2,1)} fusion(bf16[1024,512]{1,0:T(8,128)(2,1)} %param.9, bf16[512,2880]{0,1:T(8,128)(2,1)S(1)} %copy-done), kind=kOutput, calls=%fused_computation.15 | convolution fusion | flops 3022848000 | bytes 9895936 | tf_op jit(solution)/shard_map/dot_general | solution.py:22
  15.3 8.5 %copy.41 = bf16[1024,2880]{1,0:T(8,128)(2,1)} copy(bf16[1024,2880]{0,1:T(8,128)(2,1)} %convolution_convert_fusion) | data formatting | bytes 11796480
  23.9 0.7 copy-done.6
  25.0 0.2 fusion.33
  25.5 2.3 copy.34
  27.8 2.4 convert_element_type.70
  30.4 0.2 fusion.32
  30.7 14.6 %scatter_custom_fusion.1 = bf16[640,2880]{1,0:T(8,128)(2,1)} fusion(s32[512]{0:T(512)S(1)} %bitcast.55, f32[512]{0:T(512)S(1)} %mul.102, bf16[]{:T(256)} %constant.32.clone.1, f32[128,2880]{1,0:T(8,128)} %convert_element_type.70, s32[1024]{0:T(1024)S(1)} %pad_clamp_fusion.1), kind=kCustom, calls=%fused_computation.22 | custom fusion | flops 2949120 | bytes 5167106 | tf_op jit(solution)/shard_map/scatter | solution.py:46
  45.3 7.4 %reshape.152 = bf16[128,5,2880]{2,1,0:T(8,128)(2,1)} reshape(bf16[640,2880]{1,0:T(8,128)(2,1)} %scatter_custom_fusion.1) | data formatting | bytes 7372800 | tf_op jit(solution)/shard_map/reshape | solution.py:48
  52.7 12.2 %all-to-all-start.2 = ((bf16[128,5,2880]{2,1,0:T(8,128)(2,1)}), bf16[128,5,2880]{2,1,0:T(8,128)(2,1)}, u32[]{:S(2)}, u32[]{:S(2)}) async-start(bf16[128,5,2880]{2,1,0:T(8,128)(2,1)} %reshape.152), calls=%async_computation.2 | async-start | bytes 12058624 | tf_op jit(solution)/shard_map/all_to_all | solution.py:51
  65.0 2.3 copy.26
  67.3 0.6 reduce-scatter.4.cloned.1.call-done
  67.9 1.7 multiply_reduce_fusion.1
  69.6 2.5 multiply_convert_fusion.4
  72.1 23.4 %scatter_custom_fusion = bf16[640,2880]{1,0:T(8,128)(2,1)} fusion(s32[512]{0:T(512)S(1)} %bitcast.56, bf16[128,2880]{1,0:T(8,128)(2,1)} %multiply_convert_fusion.4, s32[1024]{0:T(1024)S(1)} %pad_clamp_fusion.1, bf16[]{:T(256)} %constant.32.clone.1), kind=kCustom, calls=%fused_computation.23 | custom fusion | bytes 3686912 | tf_op jit(solution)/shard_map/scatter | solution.py:44
  95.5 7.4 %reshape.147 = bf16[128,5,2880]{2,1,0:T(8,128)(2,1)} reshape(bf16[640,2880]{1,0:T(8,128)(2,1)} %scatter_custom_fusion) | data formatting | bytes 7372800 | tf_op jit(solution)/shard_map/reshape | solution.py:47
  102.9 35.3 %all-to-all-done.2 = bf16[128,5,2880]{2,1,0:T(8,128)(2,1)} async-done(((bf16[128,5,2880]{2,1,0:T(8,128)(2,1)}), bf16[128,5,2880]{2,1,0:T(8,128)(2,1)}, u32[]{:S(2)}, u32[]{:S(2)}) %all-to-all-start.2) | async-done | bytes 3686432 | tf_op jit(solution)/shard_map/all_to_all | solution.py:51
  138.2 5.4 %all-to-all-start = ((bf16[128,5,2880]{2,1,0:T(8,128)(2,1)}), bf16[128,5,2880]{2,1,0:T(8,128)(2,1)}, u32[]{:S(2)}, u32[]{:S(2)}) async-start(bf16[128,5,2880]{2,1,0:T(8,128)(2,1)} %reshape.147), calls=%async_computation | async-start | bytes 12058624 | tf_op jit(solution)/shard_map/all_to_all | solution.py:50
  143.6 7.9 %reshape.153 = bf16[640,2880]{1,0:T(8,128)(2,1)} reshape(bf16[128,5,2880]{2,1,0:T(8,128)(2,1)} %all-to-all-done.2) | data formatting | bytes 7372800 | tf_op jit(solution)/shard_map/reshape | solution.py:54
  151.5 64.6 %all-to-all-done = bf16[128,5,2880]{2,1,0:T(8,128)(2,1)} async-done(((bf16[128,5,2880]{2,1,0:T(8,128)(2,1)}), bf16[128,5,2880]{2,1,0:T(8,128)(2,1)}, u32[]{:S(2)}, u32[]{:S(2)}) %all-to-all-start) | async-done | bytes 3686432 | tf_op jit(solution)/shard_map/all_to_all | solution.py:50
  216.1 7.9 %reshape.148 = bf16[640,2880]{1,0:T(8,128)(2,1)} reshape(bf16[128,5,2880]{2,1,0:T(8,128)(2,1)} %all-to-all-done) | data formatting | bytes 7372800 | tf_op jit(solution)/shard_map/reshape | solution.py:53
  224.1 11.9 %fusion.6 = f32[640,1440]{0,1:T(8,128)} fusion(bf16[640,2880]{1,0:T(8,128)(2,1)} %reshape.148, bf16[1,2880,1440]{1,2,0:T(8,128)(2,1)} %param.13), kind=kOutput, calls=%fused_computation.12 | convolution fusion | flops 5308416000 | bytes 15667200 | tf_op jit(solution)/shard_map/dot_general | solution.py:57
  236.0 35.6 %fusion.8 = bf16[640,2880]{0,1:T(8,128)(2,1)} fusion(bf16[1,2880,1440]{1,2,0:T(8,128)(2,1)} %param.13, f32[640,1440]{0,1:T(8,128)} %fusion.6, bf16[640,2880]{1,0:T(8,128)(2,1)} %reshape.153, bf16[1,1440,2880]{2,1,0:T(8,128)(2,1)} %param.14), kind=kOutput, calls=%fused_computation.16 | convolution fusion | flops 10626969600 | bytes 27648000 | tf_op jit(solution)/shard_map/rf,df->rd/dot_general | solution.py:64
  271.6 6.2 %copy.36 = bf16[640,2880]{1,0:T(8,128)(2,1)} copy(bf16[640,2880]{0,1:T(8,128)(2,1)} %fusion.8) | data formatting | bytes 7372800 | tf_op jit(solution)/shard_map/convert_element_type | solution.py:66
  277.8 7.4 %reshape.154 = bf16[128,5,2880]{2,1,0:T(8,128)(2,1)} reshape(bf16[640,2880]{1,0:T(8,128)(2,1)} %copy.36) | data formatting | bytes 7372800 | tf_op jit(solution)/shard_map/reshape | solution.py:76
  285.1 6.0 %all-to-all-start.3 = ((bf16[128,5,2880]{2,1,0:T(8,128)(2,1)}), bf16[128,5,2880]{2,1,0:T(8,128)(2,1)}, u32[]{:S(2)}, u32[]{:S(2)}) async-start(bf16[128,5,2880]{2,1,0:T(8,128)(2,1)} %reshape.154), calls=%async_computation.3 | async-start | bytes 12058624 | tf_op jit(solution)/shard_map/all_to_all | solution.py:75
  291.2 12.6 %fusion.11 = bf16[640,2880]{0,1:T(8,128)(2,1)} fusion(bf16[1,1440,2880]{2,1,0:T(8,128)(2,1)} %param.14, f32[640,1440]{0,1:T(8,128)} %fusion.6), kind=kOutput, calls=%fused_computation.17 | convolution fusion | flops 5314867200 | bytes 15667200 | tf_op jit(solution)/shard_map/dot_general | solution.py:59
  303.7 6.1 %copy.33 = bf16[640,2880]{1,0:T(8,128)(2,1)} copy(bf16[640,2880]{0,1:T(8,128)(2,1)} %fusion.11) | data formatting | bytes 7372800 | tf_op jit(solution)/shard_map/convert_element_type | solution.py:59
  309.8 7.4 %reshape.149 = bf16[128,5,2880]{2,1,0:T(8,128)(2,1)} reshape(bf16[640,2880]{1,0:T(8,128)(2,1)} %copy.33) | data formatting | bytes 7372800 | tf_op jit(solution)/shard_map/reshape | solution.py:69
  317.2 46.3 %all-to-all-done.3 = bf16[128,5,2880]{2,1,0:T(8,128)(2,1)} async-done(((bf16[128,5,2880]{2,1,0:T(8,128)(2,1)}), bf16[128,5,2880]{2,1,0:T(8,128)(2,1)}, u32[]{:S(2)}, u32[]{:S(2)}) %all-to-all-start.3) | async-done | bytes 3686432 | tf_op jit(solution)/shard_map/all_to_all | solution.py:75
  363.4 5.5 %all-to-all-start.1 = ((bf16[128,5,2880]{2,1,0:T(8,128)(2,1)}), bf16[128,5,2880]{2,1,0:T(8,128)(2,1)}, u32[]{:S(2)}, u32[]{:S(2)}) async-start(bf16[128,5,2880]{2,1,0:T(8,128)(2,1)} %reshape.149), calls=%async_computation.1 | async-start | bytes 12058624 | tf_op jit(solution)/shard_map/all_to_all | solution.py:68
  369.0 0.2 copy.39
  369.2 7.9 %reshape.155 = bf16[640,2880]{1,0:T(8,128)(2,1)} reshape(bf16[128,5,2880]{2,1,0:T(8,128)(2,1)} %all-to-all-done.3) | data formatting | bytes 7372800 | tf_op jit(solution)/shard_map/reshape | solution.py:88
  377.2 9.3 %gather_fusion.1 = bf16[512,2880]{1,0:T(8,128)(2,1)} fusion(bf16[640,2880]{1,0:T(8,128)(2,1)} %reshape.155, s32[1024]{0:T(1024)S(1)} %pad_clamp_fusion), kind=kCustom, calls=%fused_computation.3 | custom fusion | bytes 5900288 | tf_op jit(solution)/shard_map/gather | solution.py:88
  386.4 6.5 %reshape.156 = f32[128,4,2880]{2,1,0:T(4,128)} reshape(bf16[512,2880]{1,0:T(8,128)(2,1)} %gather_fusion.1) | data formatting | bytes 8847360 | tf_op jit(solution)/shard_map/convert_element_type | solution.py:91
  392.9 7.5 %reduce_sum.51 = f32[128,2880]{1,0:T(8,128)} reduce(f32[128,4,2880]{2,1,0:T(4,128)} %reshape.156, f32[]{:T(128)} %constant.31.clone.1), dimensions={1}, to_apply=%region_8.9 | reduce | flops 1105920 | bytes 7372804 | tf_op jit(solution)/shard_map/reduce_sum | solution.py:91
  400.4 2.2 multiply_reduce_fusion
  402.6 38.8 %all-to-all-done.1 = bf16[128,5,2880]{2,1,0:T(8,128)(2,1)} async-done(((bf16[128,5,2880]{2,1,0:T(8,128)(2,1)}), bf16[128,5,2880]{2,1,0:T(8,128)(2,1)}, u32[]{:S(2)}, u32[]{:S(2)}) %all-to-all-start.1) | async-done | bytes 3686432 | tf_op jit(solution)/shard_map/all_to_all | solution.py:68
  441.4 7.9 %reshape.150 = bf16[640,2880]{1,0:T(8,128)(2,1)} reshape(bf16[128,5,2880]{2,1,0:T(8,128)(2,1)} %all-to-all-done.1) | data formatting | bytes 7372800 | tf_op jit(solution)/shard_map/reshape | solution.py:83
  449.3 9.3 %gather_fusion = bf16[512,2880]{1,0:T(8,128)(2,1)} fusion(bf16[640,2880]{1,0:T(8,128)(2,1)} %reshape.150, s32[1024]{0:T(1024)S(1)} %pad_clamp_fusion), kind=kCustom, calls=%fused_computation.1 | custom fusion | bytes 5900288 | tf_op jit(solution)/shard_map/gather | solution.py:83
  458.7 6.0 %reshape.151 = bf16[128,4,2880]{2,1,0:T(4,128)(2,1)} reshape(bf16[512,2880]{1,0:T(8,128)(2,1)} %gather_fusion) | data formatting | bytes 5898240 | tf_op jit(solution)/shard_map/reshape | solution.py:83
  464.7 3.8 fusion.39
  468.5 1.9 subtract_convert_fusion
  470.4 2.3 copy.38
  472.7 2.3 copy.37
  475.0 32.8 %all-gather.2.cloned.1.call-done = bf16[1024,2880]{1,0:T(8,128)(2,1)} async-done(((bf16[128,2880]{1,0:T(8,128)(2,1)}), bf16[1024,2880]{1,0:T(8,128)(2,1)}) %all-gather.2.cloned.1.call-update) | async-done | bytes 5898256 | tf_op jit(solution)/shard_map/all_gather | solution.py:101
  507.7 7.1 %convolution_convert_fusion.1 = bf16[1024,512]{1,0:T(8,128)(2,1)} fusion(bf16[1024,2880]{1,0:T(8,128)(2,1)} %all-gather.2.cloned.1.call-done, bf16[512,2880]{0,1:T(8,128)(2,1)S(1)} %copy-done), kind=kOutput, calls=%fused_computation.37 | convolution fusion | flops 3020423168 | bytes 9895936 | tf_op jit(solution)/shard_map/td,cd->tc/dot_general | solution.py:99
  (43 shorter events, 1.2 us)
Async XLA Ops:
  7.2 1.8 copy-start
  7.2 60.7 %reduce-scatter.4.cloned.1.call-start = ((), (), s32[]{:S(2)}) async-start(), calls=%async_computation.6 | async-start | bytes 6782976 | tf_op jit(solution)/shard_map/reduce_scatter | solution.py:21
  23.8 0.7 copy-start.6
  24.5 5.6 %copy-start.5 = (s32[128,4]{0,1:T(4,128)S(1)}, s32[128,4]{0,1:T(4,128)}, u32[]{:S(2)}) copy-start(s32[128,4]{0,1:T(4,128)} %param.16) | copy-start | bytes 6148
  52.7 14.5 %copy-start.7 = (bf16[2880]{0:T(1024)(128)(2,1)S(1)}, bf16[2880]{0:T(1024)(128)(2,1)}, u32[]{:S(2)}) copy-start(bf16[2880]{0:T(1024)(128)(2,1)} %param.12) | copy-start | bytes 17284
  52.7 85.4 %all-to-all-start.2 = ((bf16[128,5,2880]{2,1,0:T(8,128)(2,1)}), bf16[128,5,2880]{2,1,0:T(8,128)(2,1)}, u32[]{:S(2)}, u32[]{:S(2)}) async-start(bf16[128,5,2880]{2,1,0:T(8,128)(2,1)} %reshape.152), calls=%async_computation.2 | async-start | bytes 12058624 | tf_op jit(solution)/shard_map/all_to_all | solution.py:51
  138.2 78.0 %all-to-all-start = ((bf16[128,5,2880]{2,1,0:T(8,128)(2,1)}), bf16[128,5,2880]{2,1,0:T(8,128)(2,1)}, u32[]{:S(2)}, u32[]{:S(2)}) async-start(bf16[128,5,2880]{2,1,0:T(8,128)(2,1)} %reshape.147), calls=%async_computation | async-start | bytes 12058624 | tf_op jit(solution)/shard_map/all_to_all | solution.py:50
  285.1 78.3 %all-to-all-start.3 = ((bf16[128,5,2880]{2,1,0:T(8,128)(2,1)}), bf16[128,5,2880]{2,1,0:T(8,128)(2,1)}, u32[]{:S(2)}, u32[]{:S(2)}) async-start(bf16[128,5,2880]{2,1,0:T(8,128)(2,1)} %reshape.154), calls=%async_computation.3 | async-start | bytes 12058624 | tf_op jit(solution)/shard_map/all_to_all | solution.py:75
  363.4 78.0 %all-to-all-start.1 = ((bf16[128,5,2880]{2,1,0:T(8,128)(2,1)}), bf16[128,5,2880]{2,1,0:T(8,128)(2,1)}, u32[]{:S(2)}, u32[]{:S(2)}) async-start(bf16[128,5,2880]{2,1,0:T(8,128)(2,1)} %reshape.149), calls=%async_computation.1 | async-start | bytes 12058624 | tf_op jit(solution)/shard_map/all_to_all | solution.py:68
  369.0 138.7 %all-gather.2.cloned.1.call-start = ((), (), s32[]{:S(2)}) async-start(), calls=%async_computation.5 | async-start | bytes 6782976 | tf_op jit(solution)/shard_map/all_gather | solution.py:101
  464.7 3.8 copy-start.1
  464.7 3.8 copy-start.2
  464.7 3.8 copy-start.3
  464.7 3.8 copy-start.4
Sparse Core Ops, SparseCore 0:
  24.0 43.8 reduce-scatter.3
  470.6 37.1 all-gather.1
where the time goes:
time: 532 us; the launch traced here: 522 us
  waiting for transfers between devices  218 us (41%)
  local copies, waits for them, and re-layouts  149 us (28%)
  matrix products  77.2 us (15%)
  other arithmetic  33.3 us (6%)
  starting transfers between devices  29.3 us (6%)
  between operations  14.7 us (3%)
    all_to_all x1, waiting for transfers between devices, local(): lax.all_to_all(send_normed, ('expert', 'tensor'), split_axis=0, concat_ax...  64.6 us
    all_to_all x1, waiting for transfers between devices, local(): lax.all_to_all(grad_route.reshape(experts, capacity, width), ('expert', '...  46.3 us
    all_to_all x1, waiting for transfers between devices, local(): lax.all_to_all(expert_out.reshape(experts, capacity, width), ('expert', '...  38.8 us
    dot_general x1, matrix products, local(): jnp.einsum('rf,df->rd', grad_pre, up_rows, preferred_element_type=jnp.flo...  35.6 us
    all_to_all x1, waiting for transfers between devices, local(): lax.all_to_all(send_scaled, ('expert', 'tensor'), split_axis=0, concat_ax...  35.3 us
    all_gather x1, waiting for transfers between devices, local(): lax.all_gather(grad_residual, 'tensor', axis=0, tiled=True)  32.8 us
    scatter x1, local copies, waits for them, and re-layouts, local(): jnp.zeros((experts * capacity, width), jnp.bfloat16).at[positions]  23.4 us
    unnamed x23, local copies, waits for them, and re-layouts  20.2 us
  transfers between devices with their start and end apart: 6, of which 6 were waited for; matrix products, arithmetic and copies ran while one was open for 26% of the time, Pallas kernels for 0%

commit v1 on v0

v1 whole, which is shorter than its diff:
```python
import functools
import math

import jax
import jax.numpy as jnp
from jax import lax
from jax.experimental import pallas as pl
from jax.experimental.pallas import tpu as pltpu
from jax.sharding import PartitionSpec as P

CAP = 5
MESH = pl.DeviceIdType.MESH
F32, BF16 = jnp.float32, jnp.bfloat16
VMEM_LIMIT = 60 * 2**20


def chunks_of(width):
    step = -(-width // 3 // 128) * 128
    step = step + 128 if 3 * step < width else step
    return [(at, min(step, width - at)) for at in range(0, width, step)]


def tiles_of(width, step=512):
    return [(at, min(step, width - at)) for at in range(0, width, step)]


PLANE = [
    (0, 1), (1, 0), (0, 3), (3, 0), (1, 1), (3, 3), (1, 3), (3, 1),
    (0, 2), (2, 0), (1, 2), (2, 1), (3, 2), (2, 3), (2, 2),
]


class Place:
    def __init__(self):
        self.e, self.t = lax.axis_index("expert"), lax.axis_index("tensor")
        self.x, self.c = self.t // 2, lax.rem(self.t, 2)
        self.z, self.y = self.e // 4, lax.rem(self.e, 4)

    def column(self, step, other=False):
        core = 1 - self.c if other else self.c
        return lax.rem(self.x + step + 4, 4) * 2 + core

    def plane(self, offset):
        return lax.rem(self.z + offset[0], 4) * 4 + lax.rem(self.y + offset[1], 4)


class Wire:
    def __init__(self, send_sems, recv_sems):
        self.send_sems, self.recv_sems, self.count, self.sent = send_sems, recv_sems, 0, []

    def reserve(self):
        self.count += 1
        return self.count - 1

    def start(self, slot, src, dst, dev):
        copy = pltpu.make_async_remote_copy(
            src, dst, self.send_sems.at[slot], self.recv_sems.at[slot],
            device_id=dev, device_id_type=MESH,
        )
        copy.start()
        self.sent.append(copy)
        return copy

    def arrived(self, slot, landing):
        pltpu.make_async_copy(landing, landing, self.recv_sems.at[slot]).wait()

    def drain(self):
        for copy in self.sent:
            copy.wait_send()
        self.sent = []


class Gather:
    def __init__(self, place, wire, table):
        self.p, self.w, self.table = place, wire, table
        self.slots = [wire.reserve() for _ in range(8)]
        rows = table.shape[1]
        self.low, self.high = pl.ds(0, rows // 2), pl.ds(rows // 2, rows // 2)

    def begin(self):
        p, w, s, tab = self.p, self.w, self.slots, self.table
        own = tab.at[p.t]
        w.start(s[0], own, own, (p.e, p.column(1)))
        w.start(s[1], own, own, (p.e, p.column(-1)))
        w.start(s[2], own, own, (p.e, p.column(0, True)))

    def forward(self):
        p, w, s, tab = self.p, self.w, self.slots, self.table
        left, right = tab.at[p.column(-1)], tab.at[p.column(1)]
        partner = (p.e, p.column(0, True))
        w.arrived(s[0], left)
        near = tab.at[p.column(-1), self.low]
        w.start(s[3], near, near, (p.e, p.column(1)))
        w.start(s[5], left, left, partner)
        w.arrived(s[1], right)
        near = tab.at[p.column(1), self.high]
        w.start(s[4], near, near, (p.e, p.column(-1)))
        w.start(s[6], right, right, partner)

    def finish(self):
        p, w, s, tab = self.p, self.w, self.slots, self.table
        far = tab.at[p.column(2)]
        w.arrived(s[3], tab.at[p.column(2), self.low])
        w.arrived(s[4], tab.at[p.column(2), self.high])
        w.start(s[7], far, far, (p.e, p.column(0, True)))

    def settle(self):
        p, w, s, tab = self.p, self.w, self.slots, self.table
        for slot, step in ((s[2], 0), (s[5], -1), (s[6], 1), (s[7], 2)):
            w.arrived(slot, tab.at[p.column(step, True)])


class Scatter:
    def __init__(self, place, wire, part, cross, half, full):
        self.p, self.w = place, wire
        self.part, self.cross, self.half, self.full = part, cross, half, full
        self.slots = [wire.reserve() for _ in range(5)]
        rows = part.shape[2]
        self.low, self.high = pl.ds(0, rows // 2), pl.ds(rows // 2, rows // 2)

    def begin(self):
        p = self.p
        self.w.start(
            self.slots[0], self.part.at[1 - p.c], self.cross, (p.e, p.column(0, True))
        )

    def cores(self):
        p, w, s = self.p, self.w, self.slots
        w.arrived(s[0], self.cross)
        far = lax.rem(p.x + 2, 4)

        def add(at):
            mine = self.part[p.c, at].astype(F32)
            self.part[p.c, at] = (mine + self.cross[at].astype(F32)).astype(BF16)

        add(far)
        w.start(s[1], self.part.at[p.c, far, self.low], self.half.at[0], (p.e, p.column(1)))
        w.start(s[2], self.part.at[p.c, far, self.high], self.half.at[1], (p.e, p.column(-1)))
        add(lax.rem(p.x + 1, 4))
        add(lax.rem(p.x + 3, 4))
        add(p.x)

    def around(self):
        p, w, s = self.p, self.w, self.slots
        right, left = lax.rem(p.x + 1, 4), lax.rem(p.x + 3, 4)
        for slot, at, rows, side, step in (
            (0, right, self.low, 0, 1),
            (1, left, self.high, 1, -1),
        ):
            w.arrived(s[1 + slot], self.half.at[side])
            mine = self.part[p.c, at, rows].astype(F32)
            self.part[p.c, at, rows] = (mine + self.half[side].astype(F32)).astype(BF16)
            w.start(s[3 + slot], self.part.at[p.c, at], self.full.at[side], (p.e, p.column(step)))

    def result(self):
        p, w, s = self.p, self.w, self.slots
        w.arrived(s[3], self.full.at[0])
        w.arrived(s[4], self.full.at[1])
        total = self.part[p.c, p.x].astype(F32)
        return total + self.full[0].astype(F32) + self.full[1].astype(F32)


class Exchange:
    def __init__(self, place, src, dst, send_sem, recv_sem, own_sem):
        self.p, self.src, self.dst = place, src, dst
        self.sems = (send_sem, recv_sem, own_sem)

    def begin(self):
        p = self.p
        send_sem, recv_sem, own_sem = self.sems
        for offset in PLANE:
            peer = p.plane(offset)
            pltpu.make_async_remote_copy(
                self.src.at[peer], self.dst.at[p.e], send_sem, recv_sem,
                device_id=(peer, p.t), device_id_type=MESH,
            ).start()
        pltpu.make_async_copy(self.src.at[p.e], self.dst.at[p.e], own_sem).start()

    def arrived(self):
        p = self.p
        others = self.dst.at[pl.ds(0, len(PLANE))]
        pltpu.make_async_copy(others, others, self.sems[1]).wait()
        pltpu.make_async_copy(self.src.at[p.e], self.dst.at[p.e], self.sems[2]).wait()

    def drain(self):
        others = self.src.at[pl.ds(0, len(PLANE))]
        pltpu.make_async_copy(others, others, self.sems[0]).wait()


def greet(place):
    barrier = pltpu.get_barrier_semaphore()
    count = 0
    for core in (False, True):
        for step in range(4):
            if step or core:
                dev = (place.e, place.column(step, core))
                pl.semaphore_signal(barrier, inc=1, device_id=dev, device_id_type=MESH)
                count += 1
    for offset in PLANE:
        dev = (place.plane(offset), place.t)
        pl.semaphore_signal(barrier, inc=1, device_id=dev, device_id_type=MESH)
        count += 1
    pl.semaphore_wait(barrier, count)


def front_kernel(
    dims, context, out_proj, residual, gain, ids, counts, grad_out, *refs
):
    tok, width, group, slots = dims
    cuts = chunks_of(width)
    n = len(cuts)
    refs = list(refs)

    def take(k):
        out = refs[:k]
        del refs[:k]
        return out

    got_n, got_g = take(n), take(n)
    hidden, info = take(2)
    ctx, = take(1)
    proj = take(n)
    tab_n, tab_g = take(n), take(n)
    part, cross, half, full = take(n), take(n), take(n), take(n)
    out_n, out_g = take(n), take(n)
    pick, scale = take(2)
    send_sems, recv_sems, load_sems, plane_sems = refs

    p = Place()
    loads = [pltpu.make_async_copy(context, ctx, load_sems.at[0])]
    for j, (at, w) in enumerate(cuts):
        cols = pl.ds(at, w)
        loads.append(pltpu.make_async_copy(grad_out.at[:, cols], tab_g[j].at[p.t], load_sems.at[1 + j]))
    for j, (at, w) in enumerate(cuts):
        cols = pl.ds(at, w)
        loads.append(pltpu.make_async_copy(out_proj.at[:, cols], proj[j], load_sems.at[1 + n + j]))
    for load in loads:
        load.start()

    wire = Wire(send_sems, recv_sems)
    gather_g = [Gather(p, wire, tab_g[j]) for j in range(n)]
    gather_n = [Gather(p, wire, tab_n[j]) for j in range(n)]
    scatter = [Scatter(p, wire, part[j], cross[j], half[j], full[j]) for j in range(n)]
    swap_g = [Exchange(p, out_g[j], got_g[j], *(plane_sems.at[j, i] for i in range(3))) for j in range(n)]
    swap_n = [Exchange(p, out_n[j], got_n[j], *(plane_sems.at[n + j, i] for i in range(3))) for j in range(n)]
    info_slots = [wire.reserve() for _ in range(7)]

    experts = 128
    which = lax.broadcasted_iota(jnp.int32, (experts, tok), 0)
    route = [ids[k : k + 1, :] for k in range(4)]
    named = sum((which == r).astype(F32) for r in route)
    before = (
        lax.broadcasted_iota(jnp.int32, (tok, tok), 0)
        < lax.broadcasted_iota(jnp.int32, (tok, tok), 1)
    ).astype(BF16)
    earlier = jnp.dot(named.astype(BF16), before, preferred_element_type=F32)
    codes = []
    for r in route:
        rank = jnp.sum(jnp.where(which == r, earlier, 0.0), axis=0, keepdims=True)
        place = jnp.bitwise_and(r, 7) * slots + jnp.right_shift(r, 3) * group + p.t * CAP
        codes.append(place.astype(F32) + rank)
    info[p.t] = jnp.concatenate(codes + [counts[...].astype(F32)], axis=0)

    greet(p)
    for j in range(n):
        loads[1 + j].wait()
        gather_g[j].begin()
    where = [(s, c) for c in (False, True) for s in range(4) if s or c]
    for slot, (step, core) in zip(info_slots, where):
        wire.start(slot, info.at[p.t], info.at[p.t], (p.e, p.column(step, core)))
    loads[0].wait()

    def project(j):
        loads[1 + n + j].wait()
        w = cuts[j][1]

        @pl.loop(0, 4)
        def _(quarter):
            rows = pl.ds(pl.multiple_of(quarter * 2 * tok, 2 * tok), 2 * tok)
            lhs = ctx[rows, :]
            for at, size in tiles_of(w):
                got = jnp.dot(lhs, proj[j][:, at : at + size], preferred_element_type=F32)
                got = got.astype(BF16)
                part[j][0, quarter, :, at : at + size] = got[:tok]
                part[j][1, quarter, :, at : at + size] = got[tok:]

    for j in range(n):
        project(j)
        scatter[j].begin()
        gather_g[j].forward()

    for j in range(n):
        scatter[j].cores()

    for slot, (step, core) in zip(info_slots, where):
        wire.arrived(slot, info.at[p.column(-step, core)])

    @pl.loop(0, slots // 80)
    def _(block):
        first = block * 80 + p.t * slots
        slot_id = (lax.broadcasted_iota(jnp.int32, (80, tok), 0) + first).astype(F32)
        rows = pl.ds(pl.multiple_of(block * 80, 80), 80)
        weight = jnp.zeros((80, tok), F32)
        for s in range(8):
            facts = info[s]
            total = facts[4:5] + facts[5:6] + facts[6:7] + facts[7:8]
            hits = jnp.zeros((80, tok), F32)
            for k in range(4):
                hit = slot_id == facts[k : k + 1]
                hits = jnp.where(hit, 1.0, hits)
                weight = jnp.where(hit, facts[4 + k : 5 + k] / total, weight)
            pick[rows, s * tok : (s + 1) * tok] = hits.astype(BF16)
        scale[rows, :] = jnp.sum(weight, axis=1, keepdims=True)

    def select(j, table, out, weighted):
        w = cuts[j][1]
        part_rows = 8 * group

        @pl.loop(0, slots // part_rows)
        def _(block):
            rows = pl.ds(pl.multiple_of(block * part_rows, part_rows), part_rows)
            lhs = pick[rows, :]
            for at, size in tiles_of(w):
                rhs = table[:, :, at : at + size].reshape(8 * tok, size)
                got = jnp.dot(lhs, rhs, preferred_element_type=F32)
                if weighted:
                    got = got * scale[rows, :]
                out[pl.ds(block * 8, 8), :, at : at + size] = got.reshape(8, group, size).astype(BF16)

    gather_g[0].finish()
    gather_g[0].settle()
    select(0, tab_g[0], out_g[0], True)
    swap_g[0].begin()
    for j in range(n):
        scatter[j].around()
    for j in range(1, n):
        gather_g[j].finish()
    for j in range(1, n):
        gather_g[j].settle()
        select(j, tab_g[j], out_g[j], True)
        swap_g[j].begin()

    square = jnp.zeros((tok, 1), F32)
    for j, (at, w) in enumerate(cuts):
        value = residual[:, at : at + w].astype(F32) + scatter[j].result()
        hidden[:, at : at + w] = value
        square += jnp.sum(value * value, axis=1, keepdims=True)
    inv = lax.rsqrt(square / width + 1e-05)
    for j, (at, w) in enumerate(cuts):
        value = hidden[:, at : at + w] * inv * gain[:, at : at + w].astype(F32)
        tab_n[j][p.t] = value.astype(BF16)
        gather_n[j].begin()
    for j in range(n):
        gather_n[j].forward()
    for j in range(n):
        gather_n[j].finish()
        gather_n[j].settle()
        select(j, tab_n[j], out_n[j], False)
        swap_n[j].begin()
    for swap in swap_g + swap_n:
        swap.arrived()
        swap.drain()
    wire.drain()


def front(context, out_proj, residual, gain, ids, counts, grad_out, n_expert, n_tensor):
    tok, width = residual.shape
    rows, depth = context.shape
    group = n_tensor * CAP
    slots = n_expert * group
    cuts = chunks_of(width)
    n = len(cuts)
    hbm = pl.BlockSpec(memory_space=pl.ANY)
    vmem = pl.BlockSpec(memory_space=pltpu.VMEM)
    landing = [jax.ShapeDtypeStruct((n_expert, group, w), BF16) for _, w in cuts]
    per = lambda *lead: [pltpu.VMEM(lead + (w,), BF16) for _, w in cuts]
    copies = 16 * n + 5 * n + 7
    outs = pl.pallas_call(
        functools.partial(front_kernel, (tok, width, group, slots)),
        out_shape=tuple(
            landing * 2
            + [jax.ShapeDtypeStruct((tok, width), F32), jax.ShapeDtypeStruct((n_tensor, 8, tok), F32)]
        ),
        in_specs=[hbm, hbm, vmem, vmem, vmem, vmem, hbm],
        out_specs=tuple([hbm] * (2 * n) + [vmem] * 2),
        scratch_shapes=[pltpu.VMEM((rows, depth), BF16)]
        + per(depth)
        + per(n_tensor, tok) * 2
        + per(2, 4, tok)
        + per(4, tok)
        + per(2, tok // 2)
        + per(2, tok)
        + per(n_expert, group) * 2
        + [
            pltpu.VMEM((slots, n_tensor * tok), BF16),
            pltpu.VMEM((slots, 1), F32),
            pltpu.SemaphoreType.DMA((copies,)),
            pltpu.SemaphoreType.DMA((copies,)),
            pltpu.SemaphoreType.DMA((1 + 2 * n,)),
            pltpu.SemaphoreType.DMA((2 * n, 3)),
        ],
        compiler_params=pltpu.CompilerParams(
            collective_id=1, has_side_effects=True, vmem_limit_bytes=VMEM_LIMIT
        ),
        name="front",
    )(context, out_proj, residual, gain.reshape(1, width), ids, counts, grad_out)
    return outs[:n], outs[n : 2 * n], outs[2 * n], outs[2 * n + 1]


def silu_slope(pre_act):
    sigmoid_value = jax.nn.sigmoid(pre_act)
    return sigmoid_value * (1.0 + pre_act * (1.0 - sigmoid_value))


def local(
    context, out_proj, residual_in, gain, up_weight, down_weight, expert_ids, gate_counts, grad_out
):
    tok_rows, width = residual_in.shape
    n_expert = lax.axis_size("expert")
    n_tensor = lax.axis_size("tensor")
    t_me = lax.axis_index("tensor")
    group = n_tensor * CAP
    slots = n_expert * group
    got_n, got_g, hidden_in, info = front(
        context, out_proj, residual_in, gain, expert_ids.T, gate_counts.T, grad_out, n_expert, n_tensor
    )
    f32, bf16 = F32, BF16
    inputs = jnp.concatenate([a.reshape(slots, -1) for a in got_n], axis=1)
    cotangents = jnp.concatenate([a.reshape(slots, -1) for a in got_g], axis=1)
    inv_rms = lax.rsqrt(jnp.mean(hidden_in * hidden_in, axis=1, keepdims=True) + 1e-05)
    gain_f = gain.astype(f32)
    facts = info.transpose(0, 2, 1).reshape(n_tensor * tok_rows, 8)
    slot_all = facts[:, :4].astype(jnp.int32) - t_me * slots
    counts_all = facts[:, 4:]
    total_all = jnp.sum(counts_all, axis=1, keepdims=True)
    hit = slot_all[:, :, None] == jnp.arange(slots, dtype=jnp.int32)
    pick = jnp.any(hit, axis=1).astype(bf16)
    mix = jnp.sum(jnp.where(hit, counts_all[:, :, None], 0.0), axis=1).astype(bf16)

    def exchange(rows):
        return lax.all_to_all(rows, "expert", split_axis=0, concat_axis=0, tiled=True)

    up_rows = up_weight[0]
    down_rows = down_weight[0]
    pre_act = jnp.dot(inputs, up_rows, preferred_element_type=f32)
    activated = jax.nn.silu(pre_act).astype(bf16)
    expert_out = jnp.dot(activated, down_rows, preferred_element_type=f32).astype(bf16)
    back_out = exchange(expert_out)
    back_hidden = jnp.einsum("rd,fd->rf", cotangents, down_rows, preferred_element_type=f32)
    grad_pre = (back_hidden * silu_slope(pre_act)).astype(bf16)
    grad_route = jnp.einsum("rf,df->rd", grad_pre, up_rows, preferred_element_type=f32).astype(bf16)
    back_grad = exchange(grad_route)

    mix_part = (jnp.dot(mix, back_out, preferred_element_type=f32) / total_all).astype(bf16)
    expert_mix = lax.psum_scatter(mix_part, "tensor", scatter_dimension=0, tiled=True).astype(f32)
    mixed = (hidden_in + expert_mix).astype(bf16)
    grad_part = jnp.dot(pick, back_grad, preferred_element_type=f32).astype(bf16)
    grad_normed = lax.psum_scatter(grad_part, "tensor", scatter_dimension=0, tiled=True).astype(f32)
    scaled_grad = grad_normed * gain_f
    grad_hidden = (
        grad_out.astype(f32)
        + inv_rms * scaled_grad
        - hidden_in * inv_rms**3 * jnp.mean(hidden_in * scaled_grad, axis=1, keepdims=True)
    )
    grad_residual = grad_hidden.astype(bf16)
    grad_context = jnp.einsum(
        "td,cd->tc",
        lax.all_gather(grad_residual, "tensor", axis=0, tiled=True),
        out_proj,
        preferred_element_type=f32,
    ).astype(bf16)
    return (mixed, grad_residual, grad_context)


def solution(mesh):
    whole = P(("expert", "tensor"), None)
    in_specs = (
        P("expert", "tensor"),
        P("tensor", None),
        whole,
        P(),
        P(("expert", "tensor"), None, None),
        P(("expert", "tensor"), None, None),
        whole,
        whole,
        whole,
    )
    out_specs = (whole, whole, P("expert", "tensor"))
    return jax.shard_map(local, mesh=mesh, in_specs=in_specs, out_specs=out_specs, check_vma=False)
```

time: 532 us -> 462 us (0.87)
  Pallas kernels: 0 us -> 133 us
  local copies, waits for them, and re-layouts: 149 us -> 34.4 us
  waiting for transfers between devices: 218 us -> 185 us
  other arithmetic: 33.3 us -> 8.09 us
  starting transfers between devices: 29.3 us -> 9.58 us
  matrix products: 77.2 us -> 68.8 us
    pallas_call x0 -> x1, Pallas kernels: none -> 133 us  [front(): pl.pallas_call(functools.partial(front_kernel, (tok, width, group, slots)...]
    all_to_all x4 -> x2, waiting for transfers between devices: 185 us -> 110 us  [exchange(): lax.all_to_all(rows, 'expert', split_axis=0, concat_axis=0, tiled=True)]
    reshape x9 -> x1, local copies, waits for them, and re-layouts: 67.3 us -> 1.45 us  [front(): gain.reshape(1, width)]
    reduce_scatter x1 -> x2, waiting for transfers between devices: 0.62 us -> 37.4 us  [the longest x1 37.4 us: local(): lax.psum_scatter(mix_part, 'tensor', scatter_dimension=0, tiled=True)]
    scatter x1 -> x0, local copies, waits for them, and re-layouts: 23.4 us -> none  [local(): jnp.zeros((experts * capacity, width), jnp.bfloat16).at[positions]]
    all_to_all x4 -> x2, starting transfers between devices: 29.2 us -> 9.24 us  [exchange(): lax.all_to_all(rows, 'expert', split_axis=0, concat_axis=0, tiled=True)]
    gather x2 -> x0, local copies, waits for them, and re-layouts: 18.6 us -> none  [the longest x1 9.34 us: local(): back_out.reshape(experts * capacity, width)[positions]]
    scatter x1 -> x0, other arithmetic: 14.6 us -> none  [local(): jnp.zeros((experts * capacity, width), jnp.bfloat16).at[positions]]
  transfers between devices with their start and end apart: 6 -> 5, of which waited for: 6 -> 4; matrix products, arithmetic and copies ran while one was open for 26% -> 8% of each run, Pallas kernels for 0% -> 0%
where the time goes in v1:
time: 462 us; the launch traced here: 453 us
  waiting for transfers between devices  185 us (40%)
  Pallas kernels  133 us (29%)
  matrix products  68.8 us (15%)
  local copies, waits for them, and re-layouts  34.4 us (7%)
  between operations  14.2 us (3%)
  starting transfers between devices  9.58 us (2%)
  other arithmetic  8.09 us (2%)
    pallas_call x1, Pallas kernels, front(): pl.pallas_call(functools.partial(front_kernel, (tok, width, group, slots)...  133 us
    all_to_all x2, waiting for transfers between devices, exchange(): lax.all_to_all(rows, 'expert', split_axis=0, concat_axis=0, tiled=True)  110 us
    all_gather x1, waiting for transfers between devices, local(): lax.all_gather(grad_residual, 'tensor', axis=0, tiled=True)  37.5 us
    reduce_scatter x1, waiting for transfers between devices, local(): lax.psum_scatter(mix_part, 'tensor', scatter_dimension=0, tiled=True)  37.4 us
    dot_general x1, matrix products, local(): jnp.dot(activated, down_rows, preferred_element_type=f32).astype(bf16)  12.6 us
    unnamed x35, local copies, waits for them, and re-layouts  12.1 us
    dot_general x1, matrix products, local(): jnp.einsum('rf,df->rd', grad_pre, up_rows, preferred_element_type=f32)  12 us
    dot_general x1, matrix products, local(): pre_act = jnp.dot(inputs, up_rows, preferred_element_type=f32)  11.2 us
  transfers between devices with their start and end apart: 5, of which 4 were waited for; matrix products, arithmetic and copies ran while one was open for 8% of the time, Pallas kernels for 0%

profile of v1, /device:TPU:1, one launch (start us, length us, event | category | flops | bytes accessed | tf_op | source)
XLA Modules:
  0.0 453.0 jit_solution(546401215623472463)
XLA Ops:
  7.2 0.0 copy-start.2
  7.2 1.5 reshape.56.gain
  8.6 2.3 copy.44.grad_out
  10.9 2.3 copy.43.residual
  13.2 0.0 copy-done.2
  13.2 3.0 copy.42.out_proj
  16.2 132.5 %front.1 = (bf16[16,40,1024]{2,1,0:T(8,128)(2,1)}, bf16[16,40,1024]{2,1,0:T(8,128)(2,1)}, bf16[16,40,832]{2,1,0:T(8,128)(2,1)}, bf16[16,40,1024]{2,1,0:T(8,128)(...) custom-call(bf16[1024,512]{1,0:T(8,128)(2,1)} %context.1, ...), custom_call_target="tpu_custom_call" | custom-call | tf_op jit(solution)/shard_map/front/pallas_call | solution.py:378
  148.7 0.0 slice-start.4
  148.7 0.0 slice-start.5
  148.7 0.0 copy-start.5
  148.7 0.0 copy-start.6
  148.7 0.0 copy-start.7
  148.8 0.0 slice-start
  148.8 0.0 slice-start.1
  148.8 11.2 %fusion.7 = f32[640,1440]{0,1:T(8,128)S(1)} fusion(bf16[1,2880,1440]{1,2,0:T(8,128)(2,1)} %param.13, bf16[640,832]{1,0:T(8,128)(2,1)} %bitcast.55, bf16[640,1024]{1,0:T(8,128)(2,1)} %bitcast.53, bf16[640,1024]{1,0:T(8,128)(2,1)} %bitcast.52), kind=kOutput, calls=%fused_computation.10 | convolution fusion | flops 5319475200 | bytes 15667200 | tf_op jit(solution)/shard_map/dot_general | solution.py:445
  160.0 0.0 copy-start.8
  160.0 0.0 slice-done.3
  160.0 0.0 slice-done.4
  160.1 0.0 slice-start.2
  160.1 7.5 %fusion.28 = bf16[640,1440]{0,1:T(8,128)(2,1)S(1)} fusion(f32[640,1440]{0,1:T(8,128)S(1)} %fusion.7, bf16[1,1440,2880]{2,1,0:T(8,128)(2,1)S(1)} %bitcast.49, bf16[640,832]{1,0:T(8,128)(2,1)S(1)} %bitcast.54, bf16[640,1024]{1,0:T(8,128)(2,1)S(1)} %bitcast.51, bf16[640,1024]{1,0:T(8,128)(2,1)S(1)} %bitcast.50), kind=kOutput, calls=%fused_computation.28 | convolution fusion | flops 5327769600 | bytes 17510400 | tf_op jit(solution)/shard_map/rd,fd->rf/dot_general | solution.py:449
  167.6 12.0 %fusion.9 = bf16[640,2880]{0,1:T(8,128)(2,1)} fusion(bf16[640,1440]{0,1:T(8,128)(2,1)S(1)} %fusion.28, bf16[1,2880,1440]{1,2,0:T(8,128)(2,1)S(1)} %bitcast.47), kind=kOutput, calls=%fused_computation.13 | convolution fusion | flops 5310259200 | bytes 13824000 | tf_op jit(solution)/shard_map/rf,df->rd/dot_general | solution.py:451
  179.6 6.2 %copy.49 = bf16[640,2880]{1,0:T(8,128)(2,1)} copy(bf16[640,2880]{0,1:T(8,128)(2,1)} %fusion.9) | data formatting | bytes 7372800 | tf_op jit(solution)/shard_map/convert_element_type | solution.py:451
  185.8 4.7 %all-to-all-start.1 = ((bf16[16,40,2880]{2,1,0:T(8,128)(2,1)}), bf16[16,40,2880]{2,1,0:T(8,128)(2,1)}, u32[]{:S(2)}, u32[]{:S(2)}) async-start(bf16[16,40,2880]{2,1,0:T(8,128)(2,1)} %bitcast.40), calls=%async_computation.2 | async-start | bytes 7536640 | tf_op jit(solution)/shard_map/all_to_all | solution.py:441
  190.5 0.0 reduce-scatter.5.cloned.1.call-start
  190.6 1.8 fusion
  192.4 56.5 %all-to-all-done.1 = bf16[16,40,2880]{2,1,0:T(8,128)(2,1)} async-done(((bf16[16,40,2880]{2,1,0:T(8,128)(2,1)}), bf16[16,40,2880]{2,1,0:T(8,128)(2,1)}, u32[]{:S(2)}, u32[]{:S(2)}) %all-to-all-start.1) | async-done | bytes 3686432 | tf_op jit(solution)/shard_map/all_to_all | solution.py:441
  248.9 8.7 %convolution_convert_fusion = bf16[1024,2880]{0,1:T(8,128)(2,1)} fusion(pred[1024,640]{1,0:T(8,128)(4,1)S(1)} %fusion, bf16[640,2880]{1,0:T(8,128)(2,1)} %bitcast.16), kind=kOutput, calls=%fused_computation.12 | convolution fusion | flops 3777822720 | bytes 10240000 | tf_op jit(solution)/shard_map/dot_general | solution.py:457
  257.6 8.5 %copy.50 = bf16[1024,2880]{1,0:T(8,128)(2,1)} copy(bf16[1024,2880]{0,1:T(8,128)(2,1)} %convolution_convert_fusion) | data formatting | bytes 11796480 | tf_op jit(solution)/shard_map/convert_element_type | solution.py:457
  266.1 0.0 reduce-scatter.5.cloned.1.call-update
  266.2 12.6 %fusion.12 = bf16[640,2880]{0,1:T(8,128)(2,1)} fusion(bf16[1,1440,2880]{2,1,0:T(8,128)(2,1)} %param.14, f32[640,1440]{0,1:T(8,128)} %copy-done.8), kind=kOutput, calls=%fused_computation.14 | convolution fusion | flops 5314867200 | bytes 15667200 | tf_op jit(solution)/shard_map/dot_general | solution.py:447
  278.8 6.2 %copy.45 = bf16[640,2880]{1,0:T(8,128)(2,1)} copy(bf16[640,2880]{0,1:T(8,128)(2,1)} %fusion.12) | data formatting | bytes 7372800 | tf_op jit(solution)/shard_map/convert_element_type | solution.py:447
  285.0 4.5 all-to-all-start
  289.5 0.0 reduce-scatter.3.cloned.1.call-start
  289.6 1.7 select_reduce_fusion
  291.3 53.9 %all-to-all-done = bf16[16,40,2880]{2,1,0:T(8,128)(2,1)} async-done(((bf16[16,40,2880]{2,1,0:T(8,128)(2,1)}), bf16[16,40,2880]{2,1,0:T(8,128)(2,1)}, u32[]{:S(2)}, u32[]{:S(2)}) %all-to-all-start) | async-done | bytes 3686432 | tf_op jit(solution)/shard_map/all_to_all | solution.py:441
  345.2 8.8 %divide_convert_fusion = bf16[1024,2880]{1,0:T(8,128)(2,1)} fusion(f32[1024]{0:T(1024)S(1)} %get-tuple-element.36, bf16[640,2880]{1,0:T(8,128)(2,1)} %bitcast.11, bf16[1024,640]{1,0:T(8,128)(2,1)S(1)} %select_reduce_fusion), kind=kOutput, calls=%fused_computation | convolution fusion | flops 3780771840 | bytes 10899456 | tf_op jit(solution)/shard_map/dot_general | solution.py:454
  354.0 0.0 reduce-scatter.3.cloned.1.call-update
  354.0 0.3 all-gather.2.cloned.1.call-start
  354.3 0.4 copy-done.4
  354.7 0.7 copy-done.1
  355.4 1.5 multiply_reduce_fusion.1
  356.9 37.4 %reduce-scatter.3.cloned.1.call-done = bf16[128,2880]{1,0:T(8,128)(2,1)} async-done(((bf16[1024,2880]{1,0:T(8,128)(2,1)}), bf16[128,2880]{1,0:T(8,128)(2,1)}) %reduce-scatter.3.cloned.1.call-update) | async-done | bytes 737296 | tf_op jit(solution)/shard_map/reduce_scatter | solution.py:455
  394.4 3.0 subtract_convert_fusion
  397.4 0.0 all-gather.2.cloned.1.call-update
  397.4 2.3 copy.52
  399.6 1.1 copy.51
  400.8 37.5 %all-gather.2.cloned.1.call-done = bf16[1024,2880]{1,0:T(8,128)(2,1)} async-done(((bf16[128,2880]{1,0:T(8,128)(2,1)}), bf16[1024,2880]{1,0:T(8,128)(2,1)}) %all-gather.2.cloned.1.call-update) | async-done | bytes 5898256 | tf_op jit(solution)/shard_map/all_gather | solution.py:468
  438.3 8.0 %convolution_convert_fusion.1 = bf16[1024,512]{1,0:T(8,128)(2,1)} fusion(bf16[1024,2880]{1,0:T(8,128)(2,1)} %all-gather.2.cloned.1.call-done, bf16[512,2880]{0,1:T(8,128)(2,1)} %param.10), kind=kOutput, calls=%fused_computation.35 | convolution fusion | flops 3020423168 | bytes 9895936 | tf_op jit(solution)/shard_map/td,cd->tc/dot_general | solution.py:466
  (23 shorter events, 0.1 us)
Async XLA Ops:
  7.2 6.0 %copy-start.2 = (bf16[512,2880]{0,1:T(8,128)(2,1)S(1)}, bf16[512,2880]{0,1:T(8,128)(2,1)}, u32[]{:S(2)}) copy-start(bf16[512,2880]{0,1:T(8,128)(2,1)} %param.10) | copy-start | bytes 8847364
  16.2 143.8 %slice-start.3 = ((s8[8478720]{0:T(1024)(128)(4,1)}), s8[90112]{0:T(1024)(128)(4,1)S(1)}, s32[]{:S(2)}) async-start(s8[8478720]{0:T(1024)(128)(4,1)} %bitcast.48), calls=%async_computation.10 | async-start | bytes 180224
  148.7 11.3 %slice-start.4 = ((s8[8478720]{0:T(1024)(128)(4,1)}), s8[4194304]{0:T(1024)(128)(4,1)S(1)}, s32[]{:S(2)}) async-start(s8[8478720]{0:T(1024)(128)(4,1)} %bitcast.48), calls=%async_computation.11 | async-start | bytes 8388608
  148.7 11.3 %slice-start.5 = ((s8[8478720]{0:T(1024)(128)(4,1)}), s8[4194304]{0:T(1024)(128)(4,1)S(1)}, s32[]{:S(2)}) async-start(s8[8478720]{0:T(1024)(128)(4,1)} %bitcast.48), calls=%async_computation.12 | async-start | bytes 8388608
  148.7 11.3 %copy-start.5 = (bf16[16,40,1024]{2,1,0:T(8,128)(2,1)S(1)}, bf16[16,40,1024]{2,1,0:T(8,128)(2,1)}, u32[]{:S(2)}) copy-start(bf16[16,40,1024]{2,1,0:T(8,128)(2,1)} %get-tuple-element.16) | copy-start | bytes 3932164
  148.7 11.3 %copy-start.6 = (bf16[16,40,1024]{2,1,0:T(8,128)(2,1)S(1)}, bf16[16,40,1024]{2,1,0:T(8,128)(2,1)}, u32[]{:S(2)}) copy-start(bf16[16,40,1024]{2,1,0:T(8,128)(2,1)} %get-tuple-element.17) | copy-start | bytes 3932164
  148.7 11.3 %copy-start.7 = (bf16[16,40,832]{2,1,0:T(8,128)(2,1)S(1)}, bf16[16,40,832]{2,1,0:T(8,128)(2,1)}, u32[]{:S(2)}) copy-start(bf16[16,40,832]{2,1,0:T(8,128)(2,1)} %get-tuple-element.18) | copy-start | bytes 3194884
  148.8 18.9 %slice-start = ((s8[8478720]{0:T(1024)(128)(4,1)}), s8[4194304]{0:T(1024)(128)(4,1)S(1)}, s32[]{:S(2)}) async-start(s8[8478720]{0:T(1024)(128)(4,1)} %bitcast.46), calls=%async_computation.7 | async-start | bytes 8388608
  148.8 18.9 %slice-start.1 = ((s8[8478720]{0:T(1024)(128)(4,1)}), s8[4194304]{0:T(1024)(128)(4,1)S(1)}, s32[]{:S(2)}) async-start(s8[8478720]{0:T(1024)(128)(4,1)} %bitcast.46), calls=%async_computation.8 | async-start | bytes 8388608
  160.0 7.6 %copy-start.8 = (f32[640,1440]{0,1:T(8,128)}, f32[640,1440]{0,1:T(8,128)S(1)}, u32[]{:S(2)}) copy-start(f32[640,1440]{0,1:T(8,128)S(1)} %fusion.7) | copy-start | bytes 11059204
  160.1 7.6 %slice-start.2 = ((s8[8478720]{0:T(1024)(128)(4,1)}), s8[90112]{0:T(1024)(128)(4,1)S(1)}, s32[]{:S(2)}) async-start(s8[8478720]{0:T(1024)(128)(4,1)} %bitcast.46), calls=%async_computation.9 | async-start | bytes 180224
  185.8 4.8 %copy-start.3 = (f32[8,8,128]{2,1,0:T(8,128)S(1)}, f32[8,8,128]{2,1,0:T(8,128)}, u32[]{:S(2)}) copy-start(f32[8,8,128]{2,1,0:T(8,128)} %get-tuple-element.12) | copy-start | bytes 98308
  185.8 63.1 %all-to-all-start.1 = ((bf16[16,40,2880]{2,1,0:T(8,128)(2,1)}), bf16[16,40,2880]{2,1,0:T(8,128)(2,1)}, u32[]{:S(2)}, u32[]{:S(2)}) async-start(bf16[16,40,2880]{2,1,0:T(8,128)(2,1)} %bitcast.40), calls=%async_computation.2 | async-start | bytes 7536640 | tf_op jit(solution)/shard_map/all_to_all | solution.py:441
  190.5 164.2 %reduce-scatter.5.cloned.1.call-start = ((), (), s32[]{:S(2)}) async-start(), calls=%async_computation.5 | async-start | bytes 6782976 | tf_op jit(solution)/shard_map/reduce_scatter | solution.py:458
  285.0 60.3 %all-to-all-start = ((bf16[16,40,2880]{2,1,0:T(8,128)(2,1)}), bf16[16,40,2880]{2,1,0:T(8,128)(2,1)}, u32[]{:S(2)}, u32[]{:S(2)}) async-start(bf16[16,40,2880]{2,1,0:T(8,128)(2,1)} %bitcast.41), calls=%async_computation | async-start | bytes 7536640 | tf_op jit(solution)/shard_map/all_to_all | solution.py:441
  289.5 104.9 %reduce-scatter.3.cloned.1.call-start = ((), (), s32[]{:S(2)}) async-start(), calls=%async_computation.4 | async-start | bytes 6782976 | tf_op jit(solution)/shard_map/reduce_scatter | solution.py:455
  354.0 0.7 copy-start.4
  354.0 1.4 copy-start.1
  354.0 40.4 %copy-start = (bf16[128,2880]{1,0:T(8,128)(2,1)S(1)}, bf16[128,2880]{1,0:T(8,128)(2,1)}, u32[]{:S(2)}) copy-start(bf16[128,2880]{1,0:T(8,128)(2,1)} %copy.44.grad_out) | copy-start | bytes 2211844
  354.0 84.3 %all-gather.2.cloned.1.call-start = ((), (), s32[]{:S(2)}) async-start(), calls=%async_computation.6 | async-start | bytes 6782976 | tf_op jit(solution)/shard_map/all_gather | solution.py:468
Sparse Core Ops, SparseCore 0:
  266.3 38.7 reduce-scatter.4
  354.2 40.1 reduce-scatter.2
  397.5 40.7 all-gather.1

commit v2 on v1

--- a/solution.py
+++ b/solution.py
@@ -20,6 +20,10 @@
     return [(at, min(step, width - at)) for at in range(0, width, step)]
 
 
+def dot_nt(a, b):
+    return lax.dot_general(a, b, (((1,), (1,)), ((), ())), preferred_element_type=F32)
+
+
 def tiles_of(width, step=512):
     return [(at, min(step, width - at)) for at in range(0, width, step)]
 
@@ -58,56 +62,59 @@
             device_id=dev, device_id_type=MESH,
         )
         copy.start()
-        self.sent.append(copy)
-        return copy
+        self.sent.append((slot, copy))
 
     def arrived(self, slot, landing):
         pltpu.make_async_copy(landing, landing, self.recv_sems.at[slot]).wait()
 
-    def drain(self):
-        for copy in self.sent:
-            copy.wait_send()
-        self.sent = []
+    def drain(self, slots=None):
+        for slot, copy in self.sent:
+            if slots is None or slot in slots:
+                copy.wait_send()
+        self.sent = [] if slots is None else [item for item in self.sent if item[0] not in slots]
 
 
 class Gather:
-    def __init__(self, place, wire, table):
-        self.p, self.w, self.table = place, wire, table
+    def __init__(self, place, wire, table, rows):
+        self.p, self.w, self.table, self.rows = place, wire, table, rows
         self.slots = [wire.reserve() for _ in range(8)]
-        rows = table.shape[1]
-        self.low, self.high = pl.ds(0, rows // 2), pl.ds(rows // 2, rows // 2)
+
+    def block(self, index, half=None):
+        size = self.rows if half is None else self.rows // 2
+        first = index * self.rows + (half or 0) * size
+        return self.table.at[pl.ds(pl.multiple_of(first, size), size)]
 
     def begin(self):
-        p, w, s, tab = self.p, self.w, self.slots, self.table
-        own = tab.at[p.t]
+        p, w, s = self.p, self.w, self.slots
+        own = self.block(p.t)
         w.start(s[0], own, own, (p.e, p.column(1)))
         w.start(s[1], own, own, (p.e, p.column(-1)))
         w.start(s[2], own, own, (p.e, p.column(0, True)))
 
     def forward(self):
-        p, w, s, tab = self.p, self.w, self.slots, self.table
-        left, right = tab.at[p.column(-1)], tab.at[p.column(1)]
+        p, w, s = self.p, self.w, self.slots
+        left, right = self.block(p.column(-1)), self.block(p.column(1))
         partner = (p.e, p.column(0, True))
         w.arrived(s[0], left)
-        near = tab.at[p.column(-1), self.low]
+        near = self.block(p.column(-1), 0)
         w.start(s[3], near, near, (p.e, p.column(1)))
         w.start(s[5], left, left, partner)
         w.arrived(s[1], right)
-        near = tab.at[p.column(1), self.high]
+        near = self.block(p.column(1), 1)
         w.start(s[4], near, near, (p.e, p.column(-1)))
         w.start(s[6], right, right, partner)
 
     def finish(self):
-        p, w, s, tab = self.p, self.w, self.slots, self.table
-        far = tab.at[p.column(2)]
-        w.arrived(s[3], tab.at[p.column(2), self.low])
-        w.arrived(s[4], tab.at[p.column(2), self.high])
+        p, w, s = self.p, self.w, self.slots
+        far = self.block(p.column(2))
+        w.arrived(s[3], self.block(p.column(2), 0))
+        w.arrived(s[4], self.block(p.column(2), 1))
         w.start(s[7], far, far, (p.e, p.column(0, True)))
 
     def settle(self):
-        p, w, s, tab = self.p, self.w, self.slots, self.table
+        p, w, s = self.p, self.w, self.slots
         for slot, step in ((s[2], 0), (s[5], -1), (s[6], 1), (s[7], 2)):
-            w.arrived(slot, tab.at[p.column(step, True)])
+            w.arrived(slot, self.block(p.column(step, True)))
 
 
 class Scatter:
@@ -152,12 +159,16 @@
             self.part[p.c, at, rows] = (mine + self.half[side].astype(F32)).astype(BF16)
             w.start(s[3 + slot], self.part.at[p.c, at], self.full.at[side], (p.e, p.column(step)))
 
-    def result(self):
-        p, w, s = self.p, self.w, self.slots
-        w.arrived(s[3], self.full.at[0])
-        w.arrived(s[4], self.full.at[1])
-        total = self.part[p.c, p.x].astype(F32)
+    def settle(self):
+        self.w.arrived(self.slots[3], self.full.at[0])
+        self.w.arrived(self.slots[4], self.full.at[1])
+
+    def value(self):
+        total = self.part[self.p.c, self.p.x].astype(F32)
         return total + self.full[0].astype(F32) + self.full[1].astype(F32)
+
+    def release(self):
+        self.w.drain(self.slots)
 
 
 class Exchange:
@@ -229,17 +240,14 @@
     p = Place()
     loads = [pltpu.make_async_copy(context, ctx, load_sems.at[0])]
     for j, (at, w) in enumerate(cuts):
-        cols = pl.ds(at, w)
-        loads.append(pltpu.make_async_copy(grad_out.at[:, cols], tab_g[j].at[p.t], load_sems.at[1 + j]))
-    for j, (at, w) in enumerate(cuts):
-        cols = pl.ds(at, w)
-        loads.append(pltpu.make_async_copy(out_proj.at[:, cols], proj[j], load_sems.at[1 + n + j]))
+        loads.append(pltpu.make_async_copy(out_proj.at[pl.ds(at, w)], proj[j], load_sems.at[1 + j]))
     for load in loads:
         load.start()
 
     wire = Wire(send_sems, recv_sems)
-    gather_g = [Gather(p, wire, tab_g[j]) for j in range(n)]
-    gather_n = [Gather(p, wire, tab_n[j]) for j in range(n)]
+    own_rows = pl.ds(pl.multiple_of(p.t * tok, tok), tok)
+    gather_g = [Gather(p, wire, tab_g[j], tok) for j in range(n)]
+    gather_n = [Gather(p, wire, tab_n[j], tok) for j in range(n)]
     scatter = [Scatter(p, wire, part[j], cross[j], half[j], full[j]) for j in range(n)]
     swap_g = [Exchange(p, out_g[j], got_g[j], *(plane_sems.at[j, i] for i in range(3))) for j in range(n)]
     swap_n = [Exchange(p, out_n[j], got_n[j], *(plane_sems.at[n + j, i] for i in range(3))) for j in range(n)]
@@ -261,9 +269,10 @@
         codes.append(place.astype(F32) + rank)
     info[p.t] = jnp.concatenate(codes + [counts[...].astype(F32)], axis=0)
 
+    for j, (at, w) in enumerate(cuts):
+        tab_g[j][own_rows, :] = grad_out[at : at + w, :].astype(F32).T.astype(BF16)
     greet(p)
     for j in range(n):
-        loads[1 + j].wait()
         gather_g[j].begin()
     where = [(s, c) for c in (False, True) for s in range(4) if s or c]
     for slot, (step, core) in zip(info_slots, where):
@@ -271,7 +280,7 @@
     loads[0].wait()
 
     def project(j):
-        loads[1 + n + j].wait()
+        loads[1 + j].wait()
         w = cuts[j][1]
 
         @pl.loop(0, 4)
@@ -279,8 +288,7 @@
             rows = pl.ds(pl.multiple_of(quarter * 2 * tok, 2 * tok), 2 * tok)
             lhs = ctx[rows, :]
             for at, size in tiles_of(w):
-                got = jnp.dot(lhs, proj[j][:, at : at + size], preferred_element_type=F32)
-                got = got.astype(BF16)
+                got = dot_nt(lhs, proj[j][at : at + size, :]).astype(BF16)
                 part[j][0, quarter, :, at : at + size] = got[:tok]
                 part[j][1, quarter, :, at : at + size] = got[tok:]
 
@@ -321,8 +329,7 @@
             rows = pl.ds(pl.multiple_of(block * part_rows, part_rows), part_rows)
             lhs = pick[rows, :]
             for at, size in tiles_of(w):
-                rhs = table[:, :, at : at + size].reshape(8 * tok, size)
-                got = jnp.dot(lhs, rhs, preferred_element_type=F32)
+                got = jnp.dot(lhs, table[:, at : at + size], preferred_element_type=F32)
                 if weighted:
                     got = got * scale[rows, :]
                 out[pl.ds(block * 8, 8), :, at : at + size] = got.reshape(8, group, size).astype(BF16)
@@ -342,13 +349,14 @@
 
     square = jnp.zeros((tok, 1), F32)
     for j, (at, w) in enumerate(cuts):
-        value = residual[:, at : at + w].astype(F32) + scatter[j].result()
+        scatter[j].settle()
+        value = residual[at : at + w, :].astype(F32).T + scatter[j].value()
         hidden[:, at : at + w] = value
         square += jnp.sum(value * value, axis=1, keepdims=True)
     inv = lax.rsqrt(square / width + 1e-05)
     for j, (at, w) in enumerate(cuts):
         value = hidden[:, at : at + w] * inv * gain[:, at : at + w].astype(F32)
-        tab_n[j][p.t] = value.astype(BF16)
+        tab_n[j][own_rows, :] = value.astype(BF16)
         gather_n[j].begin()
     for j in range(n):
         gather_n[j].forward()
@@ -364,7 +372,7 @@
 
 
 def front(context, out_proj, residual, gain, ids, counts, grad_out, n_expert, n_tensor):
-    tok, width = residual.shape
+    width, tok = residual.shape
     rows, depth = context.shape
     group = n_tensor * CAP
     slots = n_expert * group
@@ -381,11 +389,11 @@
             landing * 2
             + [jax.ShapeDtypeStruct((tok, width), F32), jax.ShapeDtypeStruct((n_tensor, 8, tok), F32)]
         ),
-        in_specs=[hbm, hbm, vmem, vmem, vmem, vmem, hbm],
+        in_specs=[hbm, hbm, vmem, vmem, vmem, vmem, vmem],
         out_specs=tuple([hbm] * (2 * n) + [vmem] * 2),
         scratch_shapes=[pltpu.VMEM((rows, depth), BF16)]
-        + per(depth)
-        + per(n_tensor, tok) * 2
+        + [pltpu.VMEM((w, depth), BF16) for _, w in cuts]
+        + per(n_tensor * tok) * 2
         + per(2, 4, tok)
         + per(4, tok)
         + per(2, tok // 2)
@@ -396,7 +404,7 @@
             pltpu.VMEM((slots, 1), F32),
             pltpu.SemaphoreType.DMA((copies,)),
             pltpu.SemaphoreType.DMA((copies,)),
-            pltpu.SemaphoreType.DMA((1 + 2 * n,)),
+            pltpu.SemaphoreType.DMA((1 + n,)),
             pltpu.SemaphoreType.DMA((2 * n, 3)),
         ],
         compiler_params=pltpu.CompilerParams(
@@ -407,69 +415,296 @@
     return outs[:n], outs[n : 2 * n], outs[2 * n], outs[2 * n + 1]
 
 
-def silu_slope(pre_act):
-    sigmoid_value = jax.nn.sigmoid(pre_act)
-    return sigmoid_value * (1.0 + pre_act * (1.0 - sigmoid_value))
+def back_kernel(dims, inner, *refs):
+    tok, width, group, slots = dims
+    cuts = chunks_of(width)
+    n = len(cuts)
+    refs = list(refs)
+
+    def take(k):
+        out = refs[:k]
+        del refs[:k]
+        return out
+
+    got_n, got_g = take(n), take(n)
+    up_t, down, proj_t, info, hidden, gain, grad_t = take(7)
+    mixed, residual, grad_context = take(3)
+    land_o, land_g = take(n), take(n)
+    rows_n, rows_g, rows_o = take(n), take(n), take(n)
+    up, low = take(n), take(n)
+    proj, pre, act, pick, mix, total, acc = take(7)
+    part = take(n)
+    cross_o, half_o, full_o = take(n), take(n), take(n)
+    cross_g, half_g, full_g = take(n), take(n), take(n)
+    send_sems, recv_sems, load_sems, plane_sems, late_sems = refs
+
+    p = Place()
+    loads = []
+    for j, (at, w) in enumerate(cuts):
+        cols = pl.ds(at, w)
+        loads.append(
+            (
+                pltpu.make_async_copy(got_n[j], rows_n[j], load_sems.at[j, 0]),
+                pltpu.make_async_copy(up_t.at[:, cols], up[j], load_sems.at[j, 1]),
+                pltpu.make_async_copy(down.at[:, cols], low[j], load_sems.at[j, 2]),
+                pltpu.make_async_copy(got_g[j], rows_g[j], load_sems.at[j, 3]),
+            )
+        )
+    for kind in range(4):
+        for j in range(n):
+            loads[j][kind].start()
+    load_proj = pltpu.make_async_copy(proj_t, proj, load_sems.at[n, 0])
+    load_proj.start()
+
+    wire = Wire(send_sems, recv_sems)
+    sum_o = [Scatter(p, wire, part[j], cross_o[j], half_o[j], full_o[j]) for j in range(n)]
+    sum_g = [Scatter(p, wire, part[j], cross_g[j], half_g[j], full_g[j]) for j in range(n)]
+    gather = [Gather(p, wire, up[j], tok) for j in range(n)]
+    swap_o = [Exchange(p, rows_o[j], land_o[j], *(plane_sems.at[j, i] for i in range(3))) for j in range(n)]
+    swap_g = [Exchange(p, rows_n[j], land_g[j], *(plane_sems.at[n + j, i] for i in range(3))) for j in range(n)]
+
+    greet(p)
+    tiles = inner // act.shape[2]
+    depth = act.shape[2]
+    span = 8 * group
+
+    def tile_rows(i):
+        return pl.ds(pl.multiple_of(i * depth, depth), depth)
+
+    def block_rows(b):
+        return pl.ds(pl.multiple_of(b * span, span), span)
+
+    def peers(b):
+        return pl.ds(b * 8, 8)
+
+    for j in range(n):
+        loads[j][0].wait()
+        loads[j][1].wait()
+
+    @pl.loop(0, tiles)
+    def _(i):
+        @pl.loop(0, slots // span)
+        def _(b):
+            value = sum(
+                dot_nt(rows_n[j][peers(b)].reshape(span, cuts[j][1]), up[j][tile_rows(i), :])
+                for j in range(n)
+            )
+            pre[i, block_rows(b), :] = value
+            act[i, block_rows(b), :] = (value / (1.0 + jnp.exp(-value))).astype(BF16)
+
+    def widen(weight, j, out):
+        @pl.loop(0, slots // span)
+        def _(b):
+            for at, size in tiles_of(cuts[j][1]):
+                value = sum(
+                    jnp.dot(
+                        act[i, block_rows(b), :],
+                        weight[j][i * depth : (i + 1) * depth, at : at + size],
+                        preferred_element_type=F32,
+                    )
+                    for i in range(tiles)
+                )
+                out[peers(b), :, at : at + size] = value.reshape(8, group, size).astype(BF16)
+
+    for j in range(n):
+        loads[j][2].wait()
+        widen(low, j, rows_o[j])
+        swap_o[j].begin()
+
+    for j in range(n):
+        loads[j][3].wait()
+
+    @pl.loop(0, tiles)
+    def _(i):
+        @pl.loop(0, slots // span)
+        def _(b):
+            value = sum(
+                dot_nt(rows_g[j][peers(b)].reshape(span, cuts[j][1]), low[j][tile_rows(i), :])
+                for j in range(n)
+            )
+            before = pre[i, block_rows(b), :]
+            gate = 1.0 / (1.0 + jnp.exp(-before))
+            act[i, block_rows(b), :] = (value * (gate * (1.0 + before * (1.0 - gate)))).astype(BF16)
+
+    for j in range(n):
+        widen(up, j, rows_n[j])
+        swap_g[j].begin()
+
+    @pl.loop(0, 8)
+    def _(s):
+        facts = jnp.concatenate([info[s], jnp.zeros((tok - 8, tok), F32)], axis=0).T
+        slot_id = (lax.broadcasted_iota(jnp.int32, (tok, slots), 1) + p.t * slots).astype(F32)
+        hits = jnp.zeros((tok, slots), F32)
+        taken = jnp.zeros((tok, slots), F32)
+        for k in range(4):
+            hit = slot_id == facts[:, k : k + 1]
+            hits = jnp.where(hit, 1.0, hits)
+            taken = jnp.where(hit, facts[:, 4 + k : 5 + k], taken)
+        rows = pl.ds(pl.multiple_of(s * tok, tok), tok)
+        pick[rows, :] = hits.astype(BF16)
+        mix[rows, :] = taken.astype(BF16)
+        total[rows, :] = facts[:, 4:5] + facts[:, 5:6] + facts[:, 6:7] + facts[:, 7:8]
+
+    def combine(j, table, rows, shared):
+        @pl.loop(0, 4)
+        def _(quarter):
+            span2 = pl.ds(pl.multiple_of(quarter * 2 * tok, 2 * tok), 2 * tok)
+            lhs = table[span2, :]
+            for at, size in tiles_of(cuts[j][1]):
+                rhs = rows[:, :, at : at + size].reshape(slots, size)
+                value = jnp.dot(lhs, rhs, preferred_element_type=F32)
+                if shared:
+                    value = value / total[span2, :]
+                value = value.astype(BF16)
+                part[j][0, quarter, :, at : at + size] = value[:tok]
+                part[j][1, quarter, :, at : at + size] = value[tok:]
+
+    def fetch(swap, j, kind, rows):
+        swap.arrived()
+        load = pltpu.make_async_copy(swap.dst, rows, late_sems.at[j, kind])
+        load.start()
+        load.wait()
+
+    def mixed_out(j):
+        at, w = cuts[j]
+        sum_o[j].settle()
+        mixed[:, at : at + w] = (hidden[:, at : at + w] + sum_o[j].value()).astype(BF16)
+        sum_o[j].release()
+
+    for j in range(n):
+        fetch(swap_o[j], j, 0, rows_g[j])
+        combine(j, mix, rows_g[j], True)
+        sum_o[j].begin()
+        if j >= 1:
+            sum_o[j - 1].cores()
+        if j >= 2:
+            sum_o[j - 2].around()
+    sum_o[n - 1].cores()
+    for j in range(max(n - 2, 0), n):
+        sum_o[j].around()
+    for j in range(n):
+        mixed_out(j)
+
+    for j in range(n):
+        swap_o[j].drain()
+        fetch(swap_g[j], j, 1, rows_o[j])
+        combine(j, pick, rows_o[j], False)
+        sum_g[j].begin()
+        if j >= 1:
+            sum_g[j - 1].cores()
+        if j >= 2:
+            sum_g[j - 2].around()
+    sum_g[n - 1].cores()
+    for j in range(max(n - 2, 0), n):
+        sum_g[j].around()
+
+    square = jnp.zeros((tok, 1), F32)
+    cross = jnp.zeros((tok, 1), F32)
+    for j, (at, w) in enumerate(cuts):
+        sum_g[j].settle()
+        here = hidden[:, at : at + w]
+        square += jnp.sum(here * here, axis=1, keepdims=True)
+        scaled = sum_g[j].value() * gain[:, at : at + w].astype(F32)
+        cross += jnp.sum(here * scaled, axis=1, keepdims=True)
+    inv = lax.rsqrt(square / width + 1e-05)
+    slope = inv * inv * inv * (cross / width)
+    own_rows = pl.ds(pl.multiple_of(p.t * tok, tok), tok)
+    for j, (at, w) in enumerate(cuts):
+        scaled = sum_g[j].value() * gain[:, at : at + w].astype(F32)
+        value = grad_t[at : at + w, :].astype(F32).T + inv * scaled - hidden[:, at : at + w] * slope
+        value = value.astype(BF16)
+        up[j][own_rows, :] = value
+        gather[j].begin()
+        residual[:, at : at + w] = value
+    load_proj.wait()
+    for j in range(n):
+        gather[j].forward()
+    for j, (at, w) in enumerate(cuts):
+        gather[j].finish()
+        gather[j].settle()
+
+        @pl.loop(0, 4)
+        def _(quarter):
+            rows = pl.ds(pl.multiple_of(quarter * 2 * tok, 2 * tok), 2 * tok)
+            value = jnp.dot(up[j][rows, :], proj[at : at + w, :], preferred_element_type=F32)
+            if j > 0:
+                value += acc[rows, :]
+            if j < n - 1:
+                acc[rows, :] = value
+            else:
+                grad_context[rows, :] = value.astype(BF16)
+
+    for swap in swap_g:
+        swap.drain()
+    wire.drain()
+
+
+def back(got_n, got_g, up_t, down, proj_t, info, hidden, gain, grad_t, n_expert, n_tensor):
+    tok, width = hidden.shape
+    inner = down.shape[0]
+    depth = proj_t.shape[1]
+    group = n_tensor * CAP
+    slots = n_expert * group
+    cuts = chunks_of(width)
+    n = len(cuts)
+    hbm = pl.BlockSpec(memory_space=pl.ANY)
+    vmem = pl.BlockSpec(memory_space=pltpu.VMEM)
+    landing = [jax.ShapeDtypeStruct((n_expert, group, w), BF16) for _, w in cuts]
+    per = lambda *lead: [pltpu.VMEM(lead + (w,), BF16) for _, w in cuts]
+    copies = (8 + 5 + 5) * n
+    tiles = 3
+    outs = pl.pallas_call(
+        functools.partial(back_kernel, (tok, width, group, slots), inner),
+        out_shape=(
+            jax.ShapeDtypeStruct((tok, width), BF16),
+            jax.ShapeDtypeStruct((tok, width), BF16),
+            jax.ShapeDtypeStruct((n_tensor * tok, depth), BF16),
+            *landing * 2,
+        ),
+        in_specs=[hbm] * (2 * n) + [hbm, hbm, hbm, vmem, vmem, vmem, vmem],
+        out_specs=tuple([vmem] * 3 + [hbm] * (2 * n)),
+        scratch_shapes=per(n_expert, group) * 3
+        + per(inner) * 2
+        + [
+            pltpu.VMEM((width, depth), BF16),
+            pltpu.VMEM((tiles, slots, inner // tiles), F32),
+            pltpu.VMEM((tiles, slots, inner // tiles), BF16),
+            pltpu.VMEM((n_tensor * tok, slots), BF16),
+            pltpu.VMEM((n_tensor * tok, slots), BF16),
+            pltpu.VMEM((n_tensor * tok, 1), F32),
+            pltpu.VMEM((n_tensor * tok, depth), F32),
+        ]
+        + per(2, 4, tok)
+        + (per(4, tok) + per(2, tok // 2) + per(2, tok)) * 2
+        + [
+            pltpu.SemaphoreType.DMA((copies,)),
+            pltpu.SemaphoreType.DMA((copies,)),
+            pltpu.SemaphoreType.DMA((n + 1, 4)),
+            pltpu.SemaphoreType.DMA((2 * n, 3)),
+            pltpu.SemaphoreType.DMA((n, 2)),
+        ],
+        compiler_params=pltpu.CompilerParams(
+            collective_id=2, has_side_effects=True, vmem_limit_bytes=VMEM_LIMIT + 3 * 2**20
+        ),
+        name="back",
+    )(*got_n, *got_g, up_t, down, proj_t, info, hidden, gain, grad_t)
+    return outs[:3]
 
 
 def local(
     context, out_proj, residual_in, gain, up_weight, down_weight, expert_ids, gate_counts, grad_out
 ):
-    tok_rows, width = residual_in.shape
     n_expert = lax.axis_size("expert")
     n_tensor = lax.axis_size("tensor")
-    t_me = lax.axis_index("tensor")
-    group = n_tensor * CAP
-    slots = n_expert * group
+    gain_row = gain.reshape(1, -1)
     got_n, got_g, hidden_in, info = front(
-        context, out_proj, residual_in, gain, expert_ids.T, gate_counts.T, grad_out, n_expert, n_tensor
+        context, out_proj.T, residual_in.T, gain_row, expert_ids.T, gate_counts.T, grad_out.T,
+        n_expert, n_tensor,
     )
-    f32, bf16 = F32, BF16
-    inputs = jnp.concatenate([a.reshape(slots, -1) for a in got_n], axis=1)
-    cotangents = jnp.concatenate([a.reshape(slots, -1) for a in got_g], axis=1)
-    inv_rms = lax.rsqrt(jnp.mean(hidden_in * hidden_in, axis=1, keepdims=True) + 1e-05)
-    gain_f = gain.astype(f32)
-    facts = info.transpose(0, 2, 1).reshape(n_tensor * tok_rows, 8)
-    slot_all = facts[:, :4].astype(jnp.int32) - t_me * slots
-    counts_all = facts[:, 4:]
-    total_all = jnp.sum(counts_all, axis=1, keepdims=True)
-    hit = slot_all[:, :, None] == jnp.arange(slots, dtype=jnp.int32)
-    pick = jnp.any(hit, axis=1).astype(bf16)
-    mix = jnp.sum(jnp.where(hit, counts_all[:, :, None], 0.0), axis=1).astype(bf16)
-
-    def exchange(rows):
-        return lax.all_to_all(rows, "expert", split_axis=0, concat_axis=0, tiled=True)
-
-    up_rows = up_weight[0]
-    down_rows = down_weight[0]
-    pre_act = jnp.dot(inputs, up_rows, preferred_element_type=f32)
-    activated = jax.nn.silu(pre_act).astype(bf16)
-    expert_out = jnp.dot(activated, down_rows, preferred_element_type=f32).astype(bf16)
-    back_out = exchange(expert_out)
-    back_hidden = jnp.einsum("rd,fd->rf", cotangents, down_rows, preferred_element_type=f32)
-    grad_pre = (back_hidden * silu_slope(pre_act)).astype(bf16)
-    grad_route = jnp.einsum("rf,df->rd", grad_pre, up_rows, preferred_element_type=f32).astype(bf16)
-    back_grad = exchange(grad_route)
-
-    mix_part = (jnp.dot(mix, back_out, preferred_element_type=f32) / total_all).astype(bf16)
-    expert_mix = lax.psum_scatter(mix_part, "tensor", scatter_dimension=0, tiled=True).astype(f32)
-    mixed = (hidden_in + expert_mix).astype(bf16)
-    grad_part = jnp.dot(pick, back_grad, preferred_element_type=f32).astype(bf16)
-    grad_normed = lax.psum_scatter(grad_part, "tensor", scatter_dimension=0, tiled=True).astype(f32)
-    scaled_grad = grad_normed * gain_f
-    grad_hidden = (
-        grad_out.astype(f32)
-        + inv_rms * scaled_grad
-        - hidden_in * inv_rms**3 * jnp.mean(hidden_in * scaled_grad, axis=1, keepdims=True)
+    return back(
+        got_n, got_g, up_weight[0].T, down_weight[0], out_proj.T, info, hidden_in, gain_row,
+        grad_out.T, n_expert, n_tensor,
     )
-    grad_residual = grad_hidden.astype(bf16)
-    grad_context = jnp.einsum(
-        "td,cd->tc",
-        lax.all_gather(grad_residual, "tensor", axis=0, tiled=True),
-        out_proj,
-        preferred_element_type=f32,
-    ).astype(bf16)
-    return (mixed, grad_residual, grad_context)
 
 
 def solution(mesh):

time: 462 us -> 311 us (0.67); the launches traced: 453 us -> 308 us
  waiting for transfers between devices: 185 us -> 0 us
  Pallas kernels: 133 us -> 301 us
  matrix products: 68.8 us -> 0 us
  local copies, waits for them, and re-layouts: 34.4 us -> 5.81 us
  between operations: 14.2 us -> 0.66 us
  starting transfers between devices: 9.58 us -> 0 us
  other arithmetic: 8.09 us -> 0 us
    pallas_call x0 -> x1, Pallas kernels: none -> 168 us  [back(): pl.pallas_call(functools.partial(back_kernel, (tok, width, group, slots),...]
    all_to_all x2 -> x0, waiting for transfers between devices: 110 us -> none  [exchange(): lax.all_to_all(rows, 'expert', split_axis=0, concat_axis=0, tiled=True)]
    dot_general x7 -> x0, matrix products: 68.8 us -> none  [the longest x1 12.6 us: local(): jnp.dot(activated, down_rows, preferred_element_type=f32).astype(bf16)]
    all_gather x1 -> x0, waiting for transfers between devices: 37.5 us -> none  [local(): lax.all_gather(grad_residual, 'tensor', axis=0, tiled=True)]
    reduce_scatter x2 -> x0, waiting for transfers between devices: 37.4 us -> none  [the longest x1 37.4 us: local(): lax.psum_scatter(mix_part, 'tensor', scatter_dimension=0, tiled=True)]
    convert_element_type x3 -> x0, local copies, waits for them, and re-layouts: 20.9 us -> none  [the longest x1 8.51 us: local(): jnp.dot(pick, back_grad, preferred_element_type=f32).astype(bf16)]
    all_to_all x2 -> x0, starting transfers between devices: 9.24 us -> none  [exchange(): lax.all_to_all(rows, 'expert', split_axis=0, concat_axis=0, tiled=True)]
    unnamed x35 -> x7, local copies, waits for them, and re-layouts: 12.1 us -> 4.51 us
  transfers between devices with their start and end apart: 5 -> 0, of which waited for: 4 -> 0; matrix products, arithmetic and copies ran while one was open for 8% -> 0% of each run, Pallas kernels for 0% -> 0%
where the time goes in v2:
time: 311 us; the launch traced here: 308 us
  Pallas kernels  301 us (97%)
  local copies, waits for them, and re-layouts  5.81 us (2%)
    pallas_call x1, Pallas kernels, back(): pl.pallas_call(functools.partial(back_kernel, (tok, width, group, slots),...  168 us
    pallas_call x1, Pallas kernels, front(): pl.pallas_call(functools.partial(front_kernel, (tok, width, group, slots)...  133 us

profile of v2, /device:TPU:1, one launch (start us, length us, event | category | flops | bytes accessed | tf_op | source)
XLA Modules:
  0.0 307.8 jit_solution(10455369204180429728)
XLA Ops:
  0.6 1.3 reshape.9.gain.refs_11_
  1.9 132.8 %front.1 = (bf16[16,40,1024]{2,1,0:T(8,128)(2,1)}, bf16[16,40,1024]{2,1,0:T(8,128)(2,1)}, bf16[16,40,832]{2,1,0:T(8,128)(2,1)}, bf16[16,40,1024]{2,1,0:T(8,128)(...) custom-call(bf16[1024,512]{1,0:T(8,128)(2,1)} %context.1, ...), custom_call_target="tpu_custom_call" | custom-call | tf_op jit(solution)/shard_map/front/pallas_call | solution.py:386
  134.8 168.5 %back.1 = (bf16[128,2880]{1,0:T(8,128)(2,1)}, bf16[128,2880]{1,0:T(8,128)(2,1)}, bf16[1024,512]{1,0:T(8,128)(2,1)}, bf16[16,40,1024]{2,1,0:T(8,128)(2,1)}, bf16[...) custom-call(bf16[16,40,1024]{2,1,0:T(8,128)(2,1)} %get-tuple-element, ...), custom_call_target="tpu_custom_call" | custom-call | tf_op jit(solution)/shard_map/back/pallas_call | solution.py:656
  303.2 0.0 copy-start.1
  303.3 0.0 copy-start
  303.3 2.4 copy.12
  305.6 0.0 copy-done.1
  305.7 1.1 copy.13
  306.8 0.0 copy-done
  306.8 1.0 copy.15
Async XLA Ops:
  303.2 2.4 copy-start.1
  303.3 3.5 %copy-start = (bf16[1024,512]{1,0:T(8,128)(2,1)S(1)}, bf16[1024,512]{1,0:T(8,128)(2,1)}, u32[]{:S(2)}) copy-start(bf16[1024,512]{1,0:T(8,128)(2,1)} %get-tuple-element.33) | copy-start | bytes 3145732

commit v3 on v1

v3 whole, which is shorter than its diff:
```python
import functools
import math

import jax
import jax.numpy as jnp
from jax import lax
from jax.experimental import pallas as pl
from jax.experimental.pallas import tpu as pltpu
from jax.sharding import PartitionSpec as P

CAP = 5
STARTS = (0, 640, 1408, 2176)
MESH = pl.DeviceIdType.MESH
F32, BF16 = jnp.float32, jnp.bfloat16
VMEM_LIMIT = 65000 * 2**10


def chunks_of(width):
    starts = STARTS + (width,)
    return [(at, end - at) for at, end in zip(starts, starts[1:])]


def dot_nt(a, b):
    return lax.dot_general(a, b, (((1,), (1,)), ((), ())), preferred_element_type=F32)


def tiles_of(width, step=512):
    return [(at, min(step, width - at)) for at in range(0, width, step)]


PLANE = [
    (0, 1), (1, 0), (0, 3), (3, 0), (1, 1), (3, 3), (1, 3), (3, 1),
    (0, 2), (2, 0), (1, 2), (2, 1), (3, 2), (2, 3), (2, 2),
]


class Place:
    def __init__(self):
        self.e, self.t = lax.axis_index("expert"), lax.axis_index("tensor")
        self.x, self.c = self.t // 2, lax.rem(self.t, 2)
        self.z, self.y = self.e // 4, lax.rem(self.e, 4)

    def column(self, step, other=False):
        core = 1 - self.c if other else self.c
        return lax.rem(self.x + step + 4, 4) * 2 + core

    def plane(self, offset):
        return lax.rem(self.z + offset[0], 4) * 4 + lax.rem(self.y + offset[1], 4)


class Wire:
    def __init__(self, send_sems, recv_sems):
        self.send_sems, self.recv_sems, self.count, self.sent = send_sems, recv_sems, 0, []

    def reserve(self):
        self.count += 1
        return self.count - 1

    def start(self, slot, src, dst, dev):
        copy = pltpu.make_async_remote_copy(
            src, dst, self.send_sems.at[slot], self.recv_sems.at[slot],
            device_id=dev, device_id_type=MESH,
        )
        copy.start()
        self.sent.append((slot, copy))

    def arrived(self, slot, landing):
        pltpu.make_async_copy(landing, landing, self.recv_sems.at[slot]).wait()

    def drain(self, slots=None):
        for slot, copy in self.sent:
            if slots is None or slot in slots:
                copy.wait_send()
        self.sent = [] if slots is None else [item for item in self.sent if item[0] not in slots]


class Gather:
    def __init__(self, place, wire, table, rows):
        self.p, self.w, self.table, self.rows = place, wire, table, rows
        self.slots = [wire.reserve() for _ in range(8)]

    def block(self, index, half=None):
        size = self.rows if half is None else self.rows // 2
        first = index * self.rows + (half or 0) * size
        return self.table.at[pl.ds(pl.multiple_of(first, size), size)]

    def begin(self):
        p, w, s = self.p, self.w, self.slots
        own = self.block(p.t)
        w.start(s[0], own, own, (p.e, p.column(1)))
        w.start(s[1], own, own, (p.e, p.column(-1)))
        w.start(s[2], own, own, (p.e, p.column(0, True)))

    def forward(self):
        p, w, s = self.p, self.w, self.slots
        left, right = self.block(p.column(-1)), self.block(p.column(1))
        partner = (p.e, p.column(0, True))
        w.arrived(s[0], left)
        near = self.block(p.column(-1), 0)
        w.start(s[3], near, near, (p.e, p.column(1)))
        w.start(s[5], left, left, partner)
        w.arrived(s[1], right)
        near = self.block(p.column(1), 1)
        w.start(s[4], near, near, (p.e, p.column(-1)))
        w.start(s[6], right, right, partner)

    def finish(self):
        p, w, s = self.p, self.w, self.slots
        far = self.block(p.column(2))
        w.arrived(s[3], self.block(p.column(2), 0))
        w.arrived(s[4], self.block(p.column(2), 1))
        w.start(s[7], far, far, (p.e, p.column(0, True)))

    def settle(self):
        p, w, s = self.p, self.w, self.slots
        for slot, step in ((s[2], 0), (s[5], -1), (s[6], 1), (s[7], 2)):
            w.arrived(slot, self.block(p.column(step, True)))


class Scatter:
    def __init__(self, place, wire, part, cross, half, full):
        self.p, self.w = place, wire
        self.part, self.cross, self.half, self.full = part, cross, half, full
        self.slots = [wire.reserve() for _ in range(5)]
        self.rows = full.shape[1]

    def at(self, core, x, half=None):
        size = self.rows if half is None else self.rows // 2
        first = (core * 4 + x) * self.rows + (half or 0) * size
        return pl.ds(pl.multiple_of(first, size), size)

    def begin(self):
        p = self.p
        theirs = pl.ds(pl.multiple_of((1 - p.c) * 4 * self.rows, 4 * self.rows), 4 * self.rows)
        self.w.start(self.slots[0], self.part.at[theirs], self.cross, (p.e, p.column(0, True)))

    def cores(self):
        p, w, s = self.p, self.w, self.slots
        w.arrived(s[0], self.cross)
        far = lax.rem(p.x + 2, 4)

        def add(x):
            rows = self.at(p.c, x)
            theirs = pl.ds(pl.multiple_of(x * self.rows, self.rows), self.rows)
            mine = self.part[rows, :].astype(F32)
            self.part[rows, :] = (mine + self.cross[theirs, :].astype(F32)).astype(BF16)

        add(far)
        w.start(s[1], self.part.at[self.at(p.c, far, 0)], self.half.at[0], (p.e, p.column(1)))
        w.start(s[2], self.part.at[self.at(p.c, far, 1)], self.half.at[1], (p.e, p.column(-1)))
        add(lax.rem(p.x + 1, 4))
        add(lax.rem(p.x + 3, 4))
        add(p.x)

    def around(self):
        p, w, s = self.p, self.w, self.slots
        for side, step in ((0, 1), (1, -1)):
            x = lax.rem(p.x + step + 4, 4)
            w.arrived(s[1 + side], self.half.at[side])
            rows = self.at(p.c, x, side)
            mine = self.part[rows, :].astype(F32)
            self.part[rows, :] = (mine + self.half[side].astype(F32)).astype(BF16)
            w.start(
                s[3 + side], self.part.at[self.at(p.c, x)], self.full.at[side],
                (p.e, p.column(step)),
            )

    def settle(self):
        self.w.arrived(self.slots[3], self.full.at[0])
        self.w.arrived(self.slots[4], self.full.at[1])

    def value(self):
        total = self.part[self.at(self.p.c, self.p.x), :].astype(F32)
        return total + self.full[0].astype(F32) + self.full[1].astype(F32)

    def release(self):
        self.w.drain(self.slots)


class Exchange:
    def __init__(self, place, src, dst, send_sem, recv_sem, own_sem):
        self.p, self.src, self.dst = place, src, dst
        self.sems = (send_sem, recv_sem, own_sem)

    def begin(self):
        p = self.p
        send_sem, recv_sem, own_sem = self.sems
        for offset in PLANE:
            peer = p.plane(offset)
            pltpu.make_async_remote_copy(
                self.src.at[peer], self.dst.at[p.e], send_sem, recv_sem,
                device_id=(peer, p.t), device_id_type=MESH,
            ).start()
        pltpu.make_async_copy(self.src.at[p.e], self.dst.at[p.e], own_sem).start()

    def arrived(self):
        p = self.p
        others = self.dst.at[pl.ds(0, len(PLANE))]
        pltpu.make_async_copy(others, others, self.sems[1]).wait()
        pltpu.make_async_copy(self.src.at[p.e], self.dst.at[p.e], self.sems[2]).wait()

    def drain(self):
        others = self.src.at[pl.ds(0, len(PLANE))]
        pltpu.make_async_copy(others, others, self.sems[0]).wait()


def greet(place):
    barrier = pltpu.get_barrier_semaphore()
    count = 0
    for core in (False, True):
        for step in range(4):
            if step or core:
                dev = (place.e, place.column(step, core))
                pl.semaphore_signal(barrier, inc=1, device_id=dev, device_id_type=MESH)
                count += 1
    for offset in PLANE:
        dev = (place.plane(offset), place.t)
        pl.semaphore_signal(barrier, inc=1, device_id=dev, device_id_type=MESH)
        count += 1
    pl.semaphore_wait(barrier, count)


ORDER = (
    "ggB0", "P0", "P1", "P2", "saC0", "ggF0", "ggB1", "ggB2", "P3", "saC1",
    "CH", "saA0", "saC2", "ggE0", "saC3", "ggF1", "SG0", "ggF2", "saA1", "G0",
    "H0", "saA2", "saA3", "ggE1", "ggE2", "SG1", "SG2", "H1", "G1", "gnF0",
    "G2", "H2", "H3", "R", "gnF1", "RS", "gnE0", "SN0", "gnF2", "ggB3",
    "N0", "gnF3", "gnE1", "gnE2", "SN1", "SN2", "ggF3", "gnE3", "N1", "ggE3",
    "SN3", "SG3", "PK", "N2", "G3", "N3", "PARK", "FWD", "CT0", "CT1",
    "CT2", "O0", "CT3", "O1", "O2", "O3", "BH", "LO0", "B0", "B1",
    "LO1", "B2", "B3", "CO0", "CO1", "soC0", "LO2", "soC1", "soA0", "CO2",
    "soA1", "soC2", "MX0", "LO3", "CO3", "soA2", "soC3", "MX1", "LB0", "CB0",
    "soA3", "MX2", "sgC0", "sgA0", "LB1", "MX3", "CB1", "Q0", "sgC1", "grF0",
    "sgA1", "LB2", "grE0", "CB2", "AC0", "Q1", "sgC2", "LB3", "grF1", "CB3",
    "sgA2", "grE1", "sgC3", "AC1", "Q2", "sgA3", "grF2", "Q3", "M", "grE2",
    "RES", "AC2", "grF3", "grE3", "AC3", "END",
)


class Column:
    def __init__(self, ref, index, size):
        self.ref, self.index, self.size = ref, index, size

    def rows(self, key):
        if key is Ellipsis:
            return pl.ds(0, self.size)
        return key[0]

    def __getitem__(self, key):
        return self.ref[self.rows(key), self.index : self.index + 1]

    def __setitem__(self, key, value):
        self.ref[self.rows(key), self.index : self.index + 1] = value


def kernel(dims, *refs):
    tok, width, group, slots, inner = dims
    cuts = chunks_of(width)
    n = len(cuts)
    refs = list(refs)

    def take(k):
        out = refs[:k]
        del refs[:k]
        return out

    context, proj_t, res_t, gain, ids, counts, grad_t, up_t, down = take(9)
    mixed_t, residual_t, grad_context, park = take(4)
    land_g, land_o, land_b = take(n), take(n), take(n)
    rows_a, rows_b, rows_c = take(n), take(n), take(n)
    up, low = take(n), take(n)
    proj, hidden, info, pre, act, maps, cols = take(7)
    roots, root_out, root_in, slopes = take(4)
    part = take(n)
    cross_a, half_a, full_a = take(n), take(n), take(n)
    cross_b, half_b, full_b = take(n), take(n), take(n)
    send_sems, recv_sems, load_sems, plane_sems = refs

    p = Place()
    ctx = grad_context
    wire = Wire(send_sems, recv_sems)
    gather_g = [Gather(p, wire, up[j], tok) for j in range(n)]
    gather_n = [Gather(p, wire, low[j], tok) for j in range(n)]
    gather_r = [Gather(p, wire, up[j], tok) for j in range(n)]
    sum_a = [Scatter(p, wire, part[j], cross_a[j], half_a[j], full_a[j]) for j in range(n)]
    sum_o = [Scatter(p, wire, low[j], cross_b[j], half_b[j], full_b[j]) for j in range(n)]
    sum_g = [Scatter(p, wire, part[j], cross_a[j], half_a[j], full_a[j]) for j in range(n)]
    total, root_col, scale, square, cross = (
        Column(cols, i, size) for i, size in enumerate((8 * tok, 8 * tok, slots, tok, tok))
    )
    where = [(s, c) for c in (False, True) for s in range(4) if s or c]

    def everyone(table):
        reserved = [wire.reserve() for _ in where]

        def begin():
            for slot, (step, core) in zip(reserved, where):
                wire.start(slot, table.at[p.t], table.at[p.t], (p.e, p.column(step, core)))

        def settle():
            for slot, (step, core) in zip(reserved, where):
                wire.arrived(slot, table.at[p.column(-step, core)])

        return begin, settle

    info_begin, info_settle = everyone(info)
    roots_begin, roots_settle = everyone(roots)
    slopes_begin, slopes_settle = everyone(slopes)

    def exchanges(kind, src, dst):
        return [
            Exchange(p, src[j], dst[j], *(plane_sems.at[kind * n + j, i] for i in range(3)))
            for j in range(n)
        ]

    swap_g = exchanges(0, rows_a, land_g)
    swap_n = exchanges(1, rows_b, rows_c)
    swap_o = exchanges(2, rows_b, land_o)
    swap_b = exchanges(3, rows_c, land_b)
    swap_r = Exchange(p, root_out, root_in, *(plane_sems.at[4 * n, i] for i in range(3)))
    own_rows = pl.ds(pl.multiple_of(p.t * tok, tok), tok)

    def load(src, dst, j, kind):
        return pltpu.make_async_copy(src, dst, load_sems.at[j, kind])

    def row_block(index, size):
        return pl.ds(pl.multiple_of(index * size, size), size)

    span = 8 * group
    pair = 2 * tok
    depth = act.shape[2]
    tiles = inner // depth
    halves = range(slots // span)

    def peers(b):
        return pl.ds(b * 8, 8)

    def pre_rows(i, b):
        return pl.ds(pl.multiple_of(i * slots + b * span, span), span)

    def column(row):
        return jnp.broadcast_to(row, (tok, tok)).T[:, :1]

    def gain_of(j):
        at, w = cuts[j]
        return gain[:, at : at + w].astype(F32)

    def part_store(ref, quarter, at, size, value):
        ref[row_block(quarter, tok), at : at + size] = value[:tok]
        ref[row_block(4 + quarter, tok), at : at + size] = value[tok:]


    def begin_grads(j):
        gather_g[j].begin()

    def project(j):
        at_j, w = cuts[j]
        load(proj_t.at[pl.ds(at_j, w)], proj.at[pl.ds(at_j, w)], j, 0).wait()

        @pl.loop(0, 4)
        def _(quarter):
            lhs = ctx[row_block(quarter, pair), :]
            for at, size in tiles_of(w):
                got = dot_nt(lhs, proj[at_j + at : at_j + at + size, :]).astype(BF16)
                part_store(part[j], quarter, at, size, got)

        sum_a[j].begin()

    def choices():
        info_settle()

        @pl.loop(0, slots // 80)
        def _(block):
            first = block * 80 + p.t * slots
            slot_id = (lax.broadcasted_iota(jnp.int32, (80, tok), 0) + first).astype(F32)
            rows = row_block(block, 80)
            weight = jnp.zeros((80, tok), F32)
            for s in range(8):
                facts = info[s]
                whole = facts[4:5] + facts[5:6] + facts[6:7] + facts[7:8]
                hits = jnp.zeros((80, tok), F32)
                for k in range(4):
                    hit = slot_id == facts[k : k + 1]
                    hits = jnp.where(hit, 1.0, hits)
                    weight = jnp.where(hit, facts[4 + k : 5 + k] / whole, weight)
                maps[rows, s * tok : (s + 1) * tok] = hits.astype(BF16)
            scale[rows, :] = jnp.sum(weight, axis=1, keepdims=True)

    def select(j, table, out, weighted):
        @pl.loop(0, slots // span)
        def _(b):
            lhs = maps[row_block(b, span), : 8 * tok]
            for at, size in tiles_of(cuts[j][1]):
                rhs = table[: 8 * tok, at : at + size]
                got = jnp.dot(lhs, rhs, preferred_element_type=F32)
                if weighted:
                    got = got * scale[row_block(b, span), :]
                out[peers(b), :, at : at + size] = got.reshape(8, group, size).astype(BF16)

    def send_grads(j):
        gather_g[j].settle()
        select(j, up[j], rows_a[j], True)
        swap_g[j].begin()

    def project_back(j, table, first, scaled):
        at_j, w = cuts[j]

        @pl.loop(0, 4)
        def _(quarter):
            lhs = table[row_block(quarter, pair), :]
            if scaled:
                lhs = (lhs.astype(F32) * (1.0 / gain_of(j))).astype(BF16)
            value = jnp.dot(lhs, proj[at_j : at_j + w, :], preferred_element_type=F32)
            rows = row_block(first * 4 + quarter, pair)
            pre[rows, :] = value if j == 0 else pre[rows, :] + value

    def grads_back(j):
        project_back(j, up[j], 0, False)
        wire.drain(gather_g[j].slots)
        at, w = cuts[j]
        load(up_t.at[:, pl.ds(at, w)], up[j], j, 1).start()

    def hidden_chunk(j):
        at, w = cuts[j]
        sum_a[j].settle()
        value = res_t[at : at + w, :].astype(F32).T + sum_a[j].value()
        hidden[:, at : at + w] = value
        low[j][own_rows, :] = (value * gain_of(j)).astype(BF16)
        gather_n[j].begin()
        here = jnp.sum(value * value, axis=1, keepdims=True)
        square[...] = here if j == 0 else square[...] + here

    def root():
        inv = lax.rsqrt(square[...] / width + 1e-05)
        square[...] = inv
        roots[p.t] = jnp.broadcast_to(inv, (tok, tok)).T[:8]
        roots_begin()

    def send_roots():
        roots_settle()
        for s in range(8):
            root_col[s * tok : (s + 1) * tok, :] = column(roots[s][0:1])

        @pl.loop(0, slots // 80)
        def _(block):
            value = jnp.zeros((80, tok), F32)
            for s in range(8):
                hits = maps[row_block(block, 80), s * tok : (s + 1) * tok].astype(F32)
                value += hits * roots[s][0:1]
            value = jnp.sum(value, axis=1, keepdims=True)
            wide = jnp.broadcast_to(value, (80, tok)).reshape(80 // group, group, tok)
            root_out[pl.ds(block * (80 // group), 80 // group)] = wide

        swap_r.begin()

    def send_rows(j):
        gather_n[j].settle()
        select(j, low[j], rows_b[j], False)
        swap_n[j].begin()

    def rows_back(j):
        project_back(j, low[j], 1, True)
        wire.drain(gather_n[j].slots)
        at, w = cuts[j]
        load(down.at[:, pl.ds(at, w)], low[j], j, 2).start()

    def park_out():
        load(pre, park, n, 0).start()

    def picks():
        @pl.loop(0, 8)
        def _(s):
            facts = jnp.concatenate([info[s], jnp.zeros((tok - 8, tok), F32)], axis=0).T
            slot_id = (lax.broadcasted_iota(jnp.int32, (tok, slots), 1) + p.t * slots).astype(F32)
            hits = jnp.zeros((tok, slots), F32)
            taken = jnp.zeros((tok, slots), F32)
            for k in range(4):
                hit = slot_id == facts[:, k : k + 1]
                hits = jnp.where(hit, 1.0, hits)
                taken = jnp.where(hit, facts[:, 4 + k : 5 + k], taken)
            rows = row_block(s, tok)
            maps[rows, :slots] = hits.astype(BF16)
            maps[rows, slots:] = taken.astype(BF16)
            total[rows, :] = facts[:, 4:5] + facts[:, 5:6] + facts[:, 6:7] + facts[:, 7:8]

    def forward():
        load(pre, park, n, 0).wait()
        for j, (at, w) in enumerate(cuts):
            load(up_t.at[:, pl.ds(at, w)], up[j], j, 1).wait()
            swap_n[j].arrived()
            swap_n[j].drain()
        swap_r.arrived()
        swap_r.drain()

        @pl.loop(0, tiles)
        def _(i):
            @pl.loop(0, slots // span)
            def _(b):
                value = sum(
                    dot_nt(
                        rows_c[j][peers(b)].reshape(span, cuts[j][1]), up[j][row_block(i, depth), :]
                    )
                    for j in range(n)
                )
                value = value * root_in[peers(b)].reshape(span, tok)[:, :1]
                pre[pre_rows(i, b), :depth] = value
                act[i, row_block(b, span), :] = (value / (1.0 + jnp.exp(-value))).astype(BF16)

    def widen(weight, j, out):
        @pl.loop(0, slots // span)
        def _(b):
            for at, size in tiles_of(cuts[j][1]):
                value = sum(
                    jnp.dot(
                        act[i, row_block(b, span), :],
                        weight[j][i * depth : (i + 1) * depth, at : at + size],
                        preferred_element_type=F32,
                    )
                    for i in range(tiles)
                )
                out[peers(b), :, at : at + size] = value.reshape(8, group, size).astype(BF16)

    def expert_out(j):
        at, w = cuts[j]
        load(down.at[:, pl.ds(at, w)], low[j], j, 2).wait()
        widen(low, j, rows_b[j])
        swap_o[j].begin()

    def take_grads(j):
        swap_g[j].arrived()
        swap_g[j].drain()
        load(land_g[j], rows_a[j], j, 3).start()

    def backward():
        for j in range(n):
            load(land_g[j], rows_a[j], j, 3).wait()

        @pl.loop(0, tiles)
        def _(i):
            @pl.loop(0, slots // span)
            def _(b):
                value = sum(
                    dot_nt(
                        rows_a[j][peers(b)].reshape(span, cuts[j][1]), low[j][row_block(i, depth), :]
                    )
                    for j in range(n)
                )
                before = pre[pre_rows(i, b), :depth]
                gate = 1.0 / (1.0 + jnp.exp(-before))
                slope = gate * (1.0 + before * (1.0 - gate))
                act[i, row_block(b, span), :] = (value * slope).astype(BF16)

        load(park, pre, n, 1).start()

    def expert_grad(j):
        widen(up, j, rows_c[j])
        swap_b[j].begin()

    def take_out(j):
        swap_o[j].arrived()
        load(land_o[j], rows_a[j], j, 4).start()

    def take_back(j):
        swap_o[j].drain()
        swap_b[j].arrived()
        load(land_b[j], rows_b[j], j, 5).start()

    def combine(j, first, rows, ref, shared):
        @pl.loop(0, 4)
        def _(quarter):
            lhs = maps[row_block(quarter, pair), first : first + slots]
            for at, size in tiles_of(cuts[j][1]):
                rhs = rows[:, :, at : at + size].reshape(slots, size)
                value = jnp.dot(lhs, rhs, preferred_element_type=F32)
                if shared:
                    value = value / total[row_block(quarter, pair), :]
                part_store(ref, quarter, at, size, value.astype(BF16))

    def mix_chunk(j):
        load(land_o[j], rows_a[j], j, 4).wait()
        combine(j, slots, rows_a[j], low[j], True)
        sum_o[j].begin()

    def grad_chunk(j):
        load(land_b[j], rows_b[j], j, 5).wait()
        sum_a[j].release()
        combine(j, 0, rows_b[j], part[j], False)
        sum_g[j].begin()

    def mixed_out(j):
        at, w = cuts[j]
        sum_o[j].settle()
        mixed_t[at : at + w, :] = (hidden[:, at : at + w] + sum_o[j].value()).T.astype(BF16)

    def scaled_grad(j):
        at, w = cuts[j]
        sum_g[j].settle()
        scaled = sum_g[j].value() * gain_of(j)
        up[j][own_rows, :] = scaled.astype(BF16)
        gather_r[j].begin()
        here = jnp.sum(hidden[:, at : at + w] * scaled, axis=1, keepdims=True)
        cross[...] = here if j == 0 else cross[...] + here

    def slope_out():
        inv = square[...]
        cross[...] = inv * inv * inv * (cross[...] / width)
        slopes[p.t] = jnp.broadcast_to(cross[...], (tok, tok)).T[:8]
        slopes_begin()

    def residual_out():
        for j, (at, w) in enumerate(cuts):
            scaled = sum_g[j].value() * gain_of(j)
            value = square[...] * scaled - hidden[:, at : at + w] * cross[...]
            residual_t[at : at + w, :] = (grad_t[at : at + w, :].astype(F32) + value.T).astype(BF16)

    def accumulate(j):
        if j == 0:
            load(park, pre, n, 1).wait()
        gather_r[j].settle()
        at, w = cuts[j]

        @pl.loop(0, 4)
        def _(quarter):
            rows = row_block(quarter, pair)
            value = jnp.dot(up[j][rows, :], proj[at : at + w, :], preferred_element_type=F32)
            pre[rows, :] = pre[rows, :] + value * root_col[rows, :]

    def context_out():
        slopes_settle()

        @pl.loop(0, 8)
        def _(s):
            rows = row_block(s, tok)
            value = pre[rows, :] - pre[row_block(8 + s, tok), :] * column(slopes[s][0:1])
            grad_context[rows, :] = value.astype(BF16)

    by_chunk = {"ggB": begin_grads, "P": project, "SG": send_grads, "G": grads_back}
    by_chunk |= {"H": hidden_chunk, "SN": send_rows, "N": rows_back, "O": expert_out}
    by_chunk |= {"CT": take_grads, "B": expert_grad, "LO": take_out, "LB": take_back}
    by_chunk |= {"CO": mix_chunk, "CB": grad_chunk, "MX": mixed_out, "Q": scaled_grad}
    by_chunk["AC"] = accumulate
    for name, gathers in (("gg", gather_g), ("gn", gather_n), ("gr", gather_r)):
        by_chunk[name + "F"] = lambda j, of=gathers: of[j].forward()
        by_chunk[name + "E"] = lambda j, of=gathers: of[j].finish()
    for name, sums in (("sa", sum_a), ("so", sum_o), ("sg", sum_g)):
        by_chunk[name + "C"] = lambda j, of=sums: of[j].cores()
        by_chunk[name + "A"] = lambda j, of=sums: of[j].around()
    once = {"CH": choices, "R": root, "RS": send_roots, "PK": picks, "PARK": park_out}
    once |= {"FWD": forward, "BH": backward, "M": slope_out, "RES": residual_out}
    once["END"] = context_out

    load(context, ctx, n, 2).start()
    for j, (at, w) in enumerate(cuts):
        load(proj_t.at[pl.ds(at, w)], proj.at[pl.ds(at, w)], j, 0).start()
    for j, (at, w) in enumerate(cuts):
        up[j][own_rows, :] = grad_t[at : at + w, :].astype(F32).T.astype(BF16)

    experts = 128
    which = lax.broadcasted_iota(jnp.int32, (experts, tok), 0)
    route = [ids[k : k + 1, :] for k in range(4)]
    named = sum((which == r).astype(F32) for r in route)
    before = (
        lax.broadcasted_iota(jnp.int32, (tok, tok), 0)
        < lax.broadcasted_iota(jnp.int32, (tok, tok), 1)
    ).astype(BF16)
    earlier = jnp.dot(named.astype(BF16), before, preferred_element_type=F32)
    codes = []
    for r in route:
        rank = jnp.sum(jnp.where(which == r, earlier, 0.0), axis=0, keepdims=True)
        place = jnp.bitwise_and(r, 7) * slots + jnp.right_shift(r, 3) * group + p.t * CAP
        codes.append(place.astype(F32) + rank)
    info[p.t] = jnp.concatenate(codes + [counts[...].astype(F32)], axis=0)
    greet(p)
    info_begin()
    load(context, ctx, n, 2).wait()

    for step in ORDER:
        name = step.rstrip("0123456789")
        if name == step:
            once[name]()
        else:
            by_chunk[name](int(step[len(name) :]))

    for swapped in swap_b:
        swapped.drain()
    wire.drain()


def whole_block(
    context, proj_t, res_t, gain, ids, counts, grad_t, up_t, down, n_expert, n_tensor
):
    width, tok = res_t.shape
    inner = down.shape[0]
    depth = proj_t.shape[1]
    group = n_tensor * CAP
    slots = n_expert * group
    cuts = chunks_of(width)
    n = len(cuts)
    tiles = 3
    hbm = pl.BlockSpec(memory_space=pl.ANY)
    vmem = pl.BlockSpec(memory_space=pltpu.VMEM)
    landing = [jax.ShapeDtypeStruct((n_expert, group, w), BF16) for _, w in cuts]
    per = lambda *lead: [pltpu.VMEM(lead + (w,), BF16) for _, w in cuts]
    small = pltpu.VMEM((n_tensor, 8, tok), F32)
    copies = (3 * 8 + 3 * 5) * n + 3 * 7
    work_rows = max(tiles * slots, 2 * n_tensor * tok)
    outs = pl.pallas_call(
        functools.partial(kernel, (tok, width, group, slots, inner)),
        out_shape=(
            jax.ShapeDtypeStruct((width, tok), BF16),
            jax.ShapeDtypeStruct((width, tok), BF16),
            jax.ShapeDtypeStruct((n_tensor * tok, depth), BF16),
            jax.ShapeDtypeStruct((work_rows, depth), F32),
            *landing * 3,
        ),
        in_specs=[hbm, hbm] + [vmem] * 5 + [hbm, hbm],
        out_specs=tuple([vmem] * 3 + [hbm] * (1 + 3 * n)),
        scratch_shapes=per(n_expert, group) * 3
        + per(inner) * 2
        + [
            pltpu.VMEM((width, depth), BF16),
            pltpu.VMEM((tok, width), F32),
            small,
            pltpu.VMEM((work_rows, depth), F32),
            pltpu.VMEM((tiles, slots, inner // tiles), BF16),
            pltpu.VMEM((n_tensor * tok, 2 * slots), BF16),
            pltpu.VMEM((n_tensor * tok, 128), F32),
            small,
            pltpu.VMEM((n_expert, group, tok), F32),
            pltpu.VMEM((n_expert, group, tok), F32),
            small,
        ]
        + per(n_tensor * tok)
        + (per(4 * tok) + per(2, tok // 2) + per(2, tok)) * 2
        + [
            pltpu.SemaphoreType.DMA((copies,)),
            pltpu.SemaphoreType.DMA((copies,)),
            pltpu.SemaphoreType.DMA((n + 1, 6)),
            pltpu.SemaphoreType.DMA((4 * n + 1, 3)),
        ],
        compiler_params=pltpu.CompilerParams(
            collective_id=1, has_side_effects=True, vmem_limit_bytes=VMEM_LIMIT
        ),
        name="whole_block",
    )(context, proj_t, res_t, gain, ids, counts, grad_t, up_t, down)
    return outs[0].T, outs[1].T, outs[2]


def local(
    context, out_proj, residual_in, gain, up_weight, down_weight, expert_ids, gate_counts, grad_out
):
    return whole_block(
        context, out_proj.T, residual_in.T, gain.reshape(1, -1), expert_ids.T, gate_counts.T,
        grad_out.T, up_weight[0].T, down_weight[0], lax.axis_size("expert"), lax.axis_size("tensor"),
    )


def solution(mesh):
    whole = P(("expert", "tensor"), None)
    in_specs = (
        P("expert", "tensor"),
        P("tensor", None),
        whole,
        P(),
        P(("expert", "tensor"), None, None),
        P(("expert", "tensor"), None, None),
        whole,
        whole,
        whole,
    )
    out_specs = (whole, whole, P("expert", "tensor"))
    return jax.shard_map(local, mesh=mesh, in_specs=in_specs, out_specs=out_specs, check_vma=False)
```

time: 462 us -> 275 us (0.60); the launches traced: 453 us -> 274 us
  waiting for transfers between devices: 185 us -> 0 us
  Pallas kernels: 133 us -> 266 us
  matrix products: 68.8 us -> 0 us
  local copies, waits for them, and re-layouts: 34.4 us -> 7.61 us
  between operations: 14.2 us -> 0.64 us
  starting transfers between devices: 9.58 us -> 0 us
  other arithmetic: 8.09 us -> 0 us
    pallas_call x1, Pallas kernels: 133 us -> 266 us  [whole_block(): pl.pallas_call(functools.partial(kernel, (tok, width, group, slots, inner...]
    all_to_all x2 -> x0, waiting for transfers between devices: 110 us -> none  [exchange(): lax.all_to_all(rows, 'expert', split_axis=0, concat_axis=0, tiled=True)]
    dot_general x7 -> x0, matrix products: 68.8 us -> none  [the longest x1 12.6 us: local(): jnp.dot(activated, down_rows, preferred_element_type=f32).astype(bf16)]
    all_gather x1 -> x0, waiting for transfers between devices: 37.5 us -> none  [local(): lax.all_gather(grad_residual, 'tensor', axis=0, tiled=True)]
    reduce_scatter x2 -> x0, waiting for transfers between devices: 37.4 us -> none  [the longest x1 37.4 us: local(): lax.psum_scatter(mix_part, 'tensor', scatter_dimension=0, tiled=True)]
    convert_element_type x3 -> x0, local copies, waits for them, and re-layouts: 20.9 us -> none  [the longest x1 8.51 us: local(): jnp.dot(pick, back_grad, preferred_element_type=f32).astype(bf16)]
    all_to_all x2 -> x0, starting transfers between devices: 9.24 us -> none  [exchange(): lax.all_to_all(rows, 'expert', split_axis=0, concat_axis=0, tiled=True)]
    unnamed x35 -> x3, local copies, waits for them, and re-layouts: 12.1 us -> 6.31 us
  transfers between devices with their start and end apart: 5 -> 0, of which waited for: 4 -> 0; matrix products, arithmetic and copies ran while one was open for 8% -> 0% of each run, Pallas kernels for 0% -> 0%
where the time goes in v3:
time: 275 us; the launch traced here: 274 us
  Pallas kernels  266 us (97%)
  local copies, waits for them, and re-layouts  7.61 us (3%)
    pallas_call x1, Pallas kernels, whole_block(): pl.pallas_call(functools.partial(kernel, (tok, width, group, slots, inner...  266 us
    unnamed x3, local copies, waits for them, and re-layouts  6.31 us

profile of v3, /device:TPU:1, one launch (start us, length us, event | category | flops | bytes accessed | tf_op | source)
XLA Modules:
  0.0 274.3 jit_solution(3726262037712964360)
XLA Ops:
  0.6 1.3 reshape.9.refs_3_
  1.9 266.0 %whole_block.1 = (bf16[2880,128]{1,0:T(8,128)(2,1)}, bf16[2880,128]{1,0:T(8,128)(2,1)}, bf16[1024,512]{1,0:T(8,128)(2,1)}, f32[2048,512]{1,0:T(8,128)}, bf16[16,...) custom-call(bf16[1024,512]{1,0:T(8,128)(2,1)} %refs_0_.1, ...), custom_call_target="tpu_custom_call" | custom-call | tf_op jit(solution)/shard_map/whole_block/pallas_call | solution.py:707
  268.0 2.0 copy.15
  270.0 2.0 copy.16
  272.0 2.3 copy.17

commit v4 on v3

--- a/solution.py
+++ b/solution.py
@@ -9,7 +9,7 @@
 from jax.sharding import PartitionSpec as P
 
 CAP = 5
-STARTS = (0, 640, 1408, 2176)
+STARTS = (0, 512, 1024, 1792, 2432)
 MESH = pl.DeviceIdType.MESH
 F32, BF16 = jnp.float32, jnp.bfloat16
 VMEM_LIMIT = 65000 * 2**10
@@ -221,19 +221,22 @@
 
 
 ORDER = (
-    "ggB0", "P0", "P1", "P2", "saC0", "ggF0", "ggB1", "ggB2", "P3", "saC1",
-    "CH", "saA0", "saC2", "ggE0", "saC3", "ggF1", "SG0", "ggF2", "saA1", "G0",
-    "H0", "saA2", "saA3", "ggE1", "ggE2", "SG1", "SG2", "H1", "G1", "gnF0",
-    "G2", "H2", "H3", "R", "gnF1", "RS", "gnE0", "SN0", "gnF2", "ggB3",
-    "N0", "gnF3", "gnE1", "gnE2", "SN1", "SN2", "ggF3", "gnE3", "N1", "ggE3",
-    "SN3", "SG3", "PK", "N2", "G3", "N3", "PARK", "FWD", "CT0", "CT1",
-    "CT2", "O0", "CT3", "O1", "O2", "O3", "BH", "LO0", "B0", "B1",
-    "LO1", "B2", "B3", "CO0", "CO1", "soC0", "LO2", "soC1", "soA0", "CO2",
-    "soA1", "soC2", "MX0", "LO3", "CO3", "soA2", "soC3", "MX1", "LB0", "CB0",
-    "soA3", "MX2", "sgC0", "sgA0", "LB1", "MX3", "CB1", "Q0", "sgC1", "grF0",
-    "sgA1", "LB2", "grE0", "CB2", "AC0", "Q1", "sgC2", "LB3", "grF1", "CB3",
-    "sgA2", "grE1", "sgC3", "AC1", "Q2", "sgA3", "grF2", "Q3", "M", "grE2",
-    "RES", "AC2", "grF3", "grE3", "AC3", "END",
+    "ggB0", "ggB1", "P0", "P1", "ggF0", "CH", "saC0", "ggF1", "ggE0", "ggB2",
+    "saA0", "SG0", "ggE1", "saC1", "P2", "SG1", "ggF2", "P3", "H0", "ggE2",
+    "saC2", "G0", "saA1", "SG2", "gnF0", "saA2", "H1", "gnE0", "H2", "SN0",
+    "gnF1", "saC3", "N0", "P4", "G1", "gnF2", "gnE1", "saA3", "SN1", "N1",
+    "saC4", "gnE2", "G2", "H3", "saA4", "SN2", "N2", "gnF3", "H4", "gnE3",
+    "ggB3", "R", "gnF4", "SN3", "ggB4", "ggF3", "gnE4", "RS", "SN4", "ggF4",
+    "ggE3", "N3", "N4", "ggE4", "SG3", "SG4", "G3", "G4", "PARK", "FWD",
+    "O0", "O1", "CT1", "OS0", "CT0", "O2", "CT3", "O3", "OS1", "CT4",
+    "O4", "CT2", "BH", "B0", "B1", "LO0", "LO1", "PK", "CO0", "CO1",
+    "B2", "LB0", "soC0", "soC1", "CB0", "soA0", "LB1", "sgC0", "CB1", "soA1",
+    "B3", "sgA0", "B4", "sgC1", "Q0", "LB2", "sgA1", "CB2", "OS2", "grF0",
+    "MX1", "sgC2", "Q1", "grE0", "LB3", "sgA2", "CB3", "grF1", "sgC3", "LB4",
+    "OS3", "Q2", "sgA3", "CB4", "MX0", "grF2", "OS4", "sgC4", "LO2", "Q3",
+    "CO2", "sgA4", "soC2", "LO3", "grF3", "AC0", "grE2", "Q4", "CO3", "M",
+    "soA2", "LO4", "soC3", "grE1", "CO4", "grE3", "grF4", "soC4", "MX2", "soA3",
+    "AC1", "grE4", "soA4", "AC2", "AC3", "MX3", "AC4", "RES", "MX4", "END",
 )
 
 
@@ -524,6 +527,8 @@
         at, w = cuts[j]
         load(down.at[:, pl.ds(at, w)], low[j], j, 2).wait()
         widen(low, j, rows_b[j])
+
+    def send_out(j):
         swap_o[j].begin()
 
     def take_grads(j):
@@ -561,9 +566,8 @@
         load(land_o[j], rows_a[j], j, 4).start()
 
     def take_back(j):
-        swap_o[j].drain()
         swap_b[j].arrived()
-        load(land_b[j], rows_b[j], j, 5).start()
+        load(land_b[j], rows_a[j], j, 5).start()
 
     def combine(j, first, rows, ref, shared):
         @pl.loop(0, 4)
@@ -582,9 +586,9 @@
         sum_o[j].begin()
 
     def grad_chunk(j):
-        load(land_b[j], rows_b[j], j, 5).wait()
+        load(land_b[j], rows_a[j], j, 5).wait()
         sum_a[j].release()
-        combine(j, 0, rows_b[j], part[j], False)
+        combine(j, 0, rows_a[j], part[j], False)
         sum_g[j].begin()
 
     def mixed_out(j):
@@ -638,7 +642,7 @@
     by_chunk |= {"H": hidden_chunk, "SN": send_rows, "N": rows_back, "O": expert_out}
     by_chunk |= {"CT": take_grads, "B": expert_grad, "LO": take_out, "LB": take_back}
     by_chunk |= {"CO": mix_chunk, "CB": grad_chunk, "MX": mixed_out, "Q": scaled_grad}
-    by_chunk["AC"] = accumulate
+    by_chunk |= {"AC": accumulate, "OS": send_out}
     for name, gathers in (("gg", gather_g), ("gn", gather_n), ("gr", gather_r)):
         by_chunk[name + "F"] = lambda j, of=gathers: of[j].forward()
         by_chunk[name + "E"] = lambda j, of=gathers: of[j].finish()
@@ -681,7 +685,7 @@
         else:
             by_chunk[name](int(step[len(name) :]))
 
-    for swapped in swap_b:
+    for swapped in swap_o + swap_b:
         swapped.drain()
     wire.drain()
 

time: 275 us -> 235 us (0.85)
  Pallas kernels: 266 us -> 225 us
    pallas_call x1, Pallas kernels: 266 us -> 225 us  [whole_block(): pl.pallas_call(functools.partial(kernel, (tok, width, group, slots, inner...]
where the time goes in v4:
time: 235 us; the launch traced here: 233 us
  Pallas kernels  225 us (96%)
  local copies, waits for them, and re-layouts  7.61 us (3%)
    pallas_call x1, Pallas kernels, whole_block(): pl.pallas_call(functools.partial(kernel, (tok, width, group, slots, inner...  225 us
    unnamed x3, local copies, waits for them, and re-layouts  6.31 us

profile of v4, /device:TPU:1, one launch (start us, length us, event | category | flops | bytes accessed | tf_op | source)
XLA Modules:
  0.0 233.5 jit_solution(17608049941669944570)
XLA Ops:
  0.6 1.3 reshape.9.refs_3_
  1.9 225.2 %whole_block.1 = (bf16[2880,128]{1,0:T(8,128)(2,1)}, bf16[2880,128]{1,0:T(8,128)(2,1)}, bf16[1024,512]{1,0:T(8,128)(2,1)}, f32[2048,512]{1,0:T(8,128)}, bf16[16,...) custom-call(bf16[1024,512]{1,0:T(8,128)(2,1)} %refs_0_.1, ...), custom_call_target="tpu_custom_call" | custom-call | tf_op jit(solution)/shard_map/whole_block/pallas_call | solution.py:711
  227.1 2.0 copy.15
  229.2 2.0 copy.16
  231.2 2.3 copy.17

commit v5 on v4

--- a/solution.py
+++ b/solution.py
@@ -9,7 +9,7 @@
 from jax.sharding import PartitionSpec as P
 
 CAP = 5
-STARTS = (0, 512, 1024, 1792, 2432)
+STARTS = (0, 512, 1024, 1536, 2048, 2560)
 MESH = pl.DeviceIdType.MESH
 F32, BF16 = jnp.float32, jnp.bfloat16
 VMEM_LIMIT = 65000 * 2**10
@@ -221,22 +221,25 @@
 
 
 ORDER = (
-    "ggB0", "ggB1", "P0", "P1", "ggF0", "CH", "saC0", "ggF1", "ggE0", "ggB2",
-    "saA0", "SG0", "ggE1", "saC1", "P2", "SG1", "ggF2", "P3", "H0", "ggE2",
-    "saC2", "G0", "saA1", "SG2", "gnF0", "saA2", "H1", "gnE0", "H2", "SN0",
-    "gnF1", "saC3", "N0", "P4", "G1", "gnF2", "gnE1", "saA3", "SN1", "N1",
-    "saC4", "gnE2", "G2", "H3", "saA4", "SN2", "N2", "gnF3", "H4", "gnE3",
-    "ggB3", "R", "gnF4", "SN3", "ggB4", "ggF3", "gnE4", "RS", "SN4", "ggF4",
-    "ggE3", "N3", "N4", "ggE4", "SG3", "SG4", "G3", "G4", "PARK", "FWD",
-    "O0", "O1", "CT1", "OS0", "CT0", "O2", "CT3", "O3", "OS1", "CT4",
-    "O4", "CT2", "BH", "B0", "B1", "LO0", "LO1", "PK", "CO0", "CO1",
-    "B2", "LB0", "soC0", "soC1", "CB0", "soA0", "LB1", "sgC0", "CB1", "soA1",
-    "B3", "sgA0", "B4", "sgC1", "Q0", "LB2", "sgA1", "CB2", "OS2", "grF0",
-    "MX1", "sgC2", "Q1", "grE0", "LB3", "sgA2", "CB3", "grF1", "sgC3", "LB4",
-    "OS3", "Q2", "sgA3", "CB4", "MX0", "grF2", "OS4", "sgC4", "LO2", "Q3",
-    "CO2", "sgA4", "soC2", "LO3", "grF3", "AC0", "grE2", "Q4", "CO3", "M",
-    "soA2", "LO4", "soC3", "grE1", "CO4", "grE3", "grF4", "soC4", "MX2", "soA3",
-    "AC1", "grE4", "soA4", "AC2", "AC3", "MX3", "AC4", "RES", "MX4", "END",
+    "ggB0", "P0", "ggB1", "ggF0", "saC0", "ggB2", "P1", "CH", "P2", "ggF1",
+    "saC1", "P3", "ggF2", "ggE1", "saA0", "saC2", "ggE0", "SG1", "ggE2", "saA1",
+    "saA2", "H0", "SG0", "P4", "SG2", "H1", "H2", "gnF0", "saC3", "P5",
+    "gnF2", "gnE0", "saC4", "gnF1", "G0", "saA3", "SN0", "saC5", "saA4", "gnE2",
+    "gnE1", "SN2", "H3", "saA5", "N0", "SN1", "gnF3", "H4", "G1", "N1",
+    "gnE3", "H5", "R", "ggB3", "N2", "SN3", "gnF4", "G2", "gnF5", "N3",
+    "ggB4", "gnE4", "RS", "ggB5", "gnE5", "ggF3", "SN4", "ggF4", "ggF5", "N4",
+    "ggE3", "SN5", "N5", "ggE4", "SG3", "ggE5", "G3", "SG4", "SG5", "G4",
+    "G5", "PARK", "FWD", "CT3", "O0", "CT2", "O1", "O2", "O3", "O4",
+    "OS0", "CT4", "CT0", "OS1", "O5", "CT1", "CT5", "BH", "B0", "LO0",
+    "PK", "B1", "LO1", "CO0", "CO1", "B2", "B3", "LB0", "soC1", "soC0",
+    "CB0", "soA1", "B4", "sgC0", "soA0", "LB1", "CB1", "sgA0", "B5", "MX1",
+    "sgC1", "LB2", "Q0", "CB2", "sgA1", "OS2", "OS3", "LB3", "sgC2", "grF0",
+    "CB3", "Q1", "sgC3", "sgA2", "LB4", "sgA3", "Q2", "CB4", "LB5", "OS4",
+    "Q3", "OS5", "CB5", "MX0", "grF1", "LO2", "grF2", "sgC4", "sgC5", "CO2",
+    "grF3", "sgA4", "sgA5", "LO3", "grE1", "grE0", "soC2", "CO3", "Q4", "soC3",
+    "soA2", "LO4", "CO4", "grE2", "grF4", "Q5", "LO5", "CO5", "AC0", "soC4",
+    "soA3", "AC1", "soC5", "grE3", "grF5", "soA4", "grE4", "M", "AC2", "MX2",
+    "AC3", "grE5", "soA5", "RES", "AC4", "MX4", "AC5", "MX3", "MX5", "END",
 )
 
 
@@ -346,7 +349,7 @@
 
     def gain_of(j):
         at, w = cuts[j]
-        return gain[:, at : at + w].astype(F32)
+        return gain[at : at + w].astype(F32).reshape(1, w)
 
     def part_store(ref, quarter, at, size, value):
         ref[row_block(quarter, tok), at : at + size] = value[:tok]
@@ -656,8 +659,16 @@
     load(context, ctx, n, 2).start()
     for j, (at, w) in enumerate(cuts):
         load(proj_t.at[pl.ds(at, w)], proj.at[pl.ds(at, w)], j, 0).start()
-    for j, (at, w) in enumerate(cuts):
+
+    def own_grads(j):
+        at, w = cuts[j]
         up[j][own_rows, :] = grad_t[at : at + w, :].astype(F32).T.astype(BF16)
+
+    own_grads(0)
+    greet(p)
+    begin_grads(0)
+    for j in range(1, n):
+        own_grads(j)
 
     experts = 128
     which = lax.broadcasted_iota(jnp.int32, (experts, tok), 0)
@@ -674,11 +685,10 @@
         place = jnp.bitwise_and(r, 7) * slots + jnp.right_shift(r, 3) * group + p.t * CAP
         codes.append(place.astype(F32) + rank)
     info[p.t] = jnp.concatenate(codes + [counts[...].astype(F32)], axis=0)
-    greet(p)
     info_begin()
     load(context, ctx, n, 2).wait()
 
-    for step in ORDER:
+    for step in ORDER[1:]:
         name = step.rstrip("0123456789")
         if name == step:
             once[name]()
@@ -754,7 +764,7 @@
     context, out_proj, residual_in, gain, up_weight, down_weight, expert_ids, gate_counts, grad_out
 ):
     return whole_block(
-        context, out_proj.T, residual_in.T, gain.reshape(1, -1), expert_ids.T, gate_counts.T,
+        context, out_proj.T, residual_in.T, gain, expert_ids.T, gate_counts.T,
         grad_out.T, up_weight[0].T, down_weight[0], lax.axis_size("expert"), lax.axis_size("tensor"),
     )
 

time: 235 us -> 234 us (level)
  no operation moved by 1% of the time
where the time goes in v5:
time: 234 us; the launch traced here: 232 us
  Pallas kernels  225 us (96%)
  local copies, waits for them, and re-layouts  6.31 us (3%)
    pallas_call x1, Pallas kernels, whole_block(): pl.pallas_call(functools.partial(kernel, (tok, width, group, slots, inner...  225 us
    unnamed x3, local copies, waits for them, and re-layouts  6.31 us

profile of v5, /device:TPU:1, one launch (start us, length us, event | category | flops | bytes accessed | tf_op | source)
XLA Modules:
  0.0 231.7 jit_solution(14446085707067640303)
XLA Ops:
  0.6 224.8 %whole_block.1 = (bf16[2880,128]{1,0:T(8,128)(2,1)}, bf16[2880,128]{1,0:T(8,128)(2,1)}, bf16[1024,512]{1,0:T(8,128)(2,1)}, f32[2048,512]{1,0:T(8,128)}, bf16[16,...) custom-call(bf16[1024,512]{1,0:T(8,128)(2,1)} %refs_0_.1, ...), custom_call_target="tpu_custom_call" | custom-call | tf_op jit(solution)/shard_map/whole_block/pallas_call | solution.py:721
  225.4 2.0 copy.15
  227.4 2.0 copy.16
  229.5 2.3 copy.17
